TPU v7x, 256 devices: a whole 4x4x8 slice. The times are simulated.
256 devices in a mesh: row: 16 (over z_lo, x, core), col: 16 (over z_hi, y).
Axes of the slice: x: 4, y: 4, z: 8 (z_hi: 4, z_lo: 2; z = z_hi * 2 + z_lo), core: 2. Of those that a mesh axis runs over, the one named last changes fastest.
Arguments:
- tokens: bfloat16 [512, 8192], P('col', 'row'), may hold values from -6 to 6
- out_grad: bfloat16 [512, 8192], P('col', 'row'), may hold values from -6 to 6
- seq_ids: int32 [512], P('col'), may hold values from 0 to 7, never falling along the last dimension, each value on 1 to 128 neighbouring positions
- confidence: int32 [8], replicated, may hold values from 1 to 8
- gate_weight: bfloat16 [8192, 28672], P('row', 'col'), may hold values from -0.0625 to 0.0625
- up_weight: bfloat16 [8192, 28672], P('row', 'col'), may hold values from -0.0625 to 0.0625
- down_weight: bfloat16 [28672, 8192], P('col', 'row'), may hold values from -0.03125 to 0.03125
Outputs:
- grad_tokens: bfloat16 [512, 8192], P('col', 'row')
- grad_gate: bfloat16 [8192, 28672], P('row', 'col')
- grad_up: bfloat16 [8192, 28672], P('row', 'col')
- grad_down: bfloat16 [28672, 8192], P('col', 'row')
Inputs may be any that keep to these rules, and one draw needn't show every extreme that they name: `seq_ids`: sequence numbers never fall along the tokens; each sequence has 1 to 128 tokens.
All inputs are finite; a program needn't handle non-finite values.
Results may differ from a plain program's by a relative error of at most 0.0054.
Values may be sent and summed in bfloat16 or wider, within the bound.
A program may use at most 128 MiB of HBM per device.

v0:
```python
import jax
import jax.numpy as jnp
from jax import lax
from jax.sharding import PartitionSpec as P


def pointwise(gate, up, grad_hidden):
    sig = jax.nn.sigmoid(gate)
    silu_gate = gate * sig
    hidden = (silu_gate * up).astype(jnp.bfloat16)
    grad_pre_gate = (grad_hidden * up * sig * (1.0 + gate * (1.0 - sig))).astype(jnp.bfloat16)
    grad_pre_up = (grad_hidden * silu_gate).astype(jnp.bfloat16)
    return (hidden, grad_pre_gate, grad_pre_up)


def contract_rows(left, right):
    return lax.dot_general(
        left, right, (((0,), (0,)), ((), ())), preferred_element_type=jnp.float32
    )


def contract_cols(left, right):
    return lax.dot_general(
        left, right, (((1,), (1,)), ((), ())), preferred_element_type=jnp.float32
    )


def local(tokens, out_grad, seq_ids, confidence, gate_weight, up_weight, down_weight):
    levels = jnp.arange(confidence.shape[0], dtype=jnp.int32)
    onehot = (seq_ids[:, None] == levels[None, :]).astype(jnp.float32)
    factor = jnp.dot(onehot, confidence.astype(jnp.float32)) / 4.0
    weighted = (out_grad.astype(jnp.float32) * factor[:, None]).astype(jnp.bfloat16)
    all_tokens, all_weighted = (
        lax.all_gather(tokens, "col", axis=0, tiled=True),
        lax.all_gather(weighted, "col", axis=0, tiled=True),
    )
    width = gate_weight.shape[1]
    gate_part = jnp.dot(all_tokens, gate_weight, preferred_element_type=jnp.float32)
    up_part = jnp.dot(all_tokens, up_weight, preferred_element_type=jnp.float32)
    hidden_part = contract_cols(all_weighted, down_weight)
    sums = lax.psum_scatter(
        jnp.concatenate([gate_part, up_part, hidden_part], axis=1),
        "row",
        scatter_dimension=0,
        tiled=True,
    )
    hidden, grad_pre_gate, grad_pre_up = pointwise(
        sums[:, :width], sums[:, width : 2 * width], sums[:, 2 * width :]
    )
    hidden, grad_pre_gate, grad_pre_up = (
        lax.all_gather(hidden, "row", axis=0, tiled=True),
        lax.all_gather(grad_pre_gate, "row", axis=0, tiled=True),
        lax.all_gather(grad_pre_up, "row", axis=0, tiled=True),
    )
    grad_down = contract_rows(hidden, all_weighted).astype(jnp.bfloat16)
    grad_gate = contract_rows(all_tokens, grad_pre_gate).astype(jnp.bfloat16)
    grad_up = contract_rows(all_tokens, grad_pre_up).astype(jnp.bfloat16)
    grad_tokens = lax.psum_scatter(
        contract_cols(grad_pre_gate, gate_weight) + contract_cols(grad_pre_up, up_weight),
        "col",
        scatter_dimension=0,
        tiled=True,
    ).astype(jnp.bfloat16)
    return (grad_tokens, grad_gate, grad_up, grad_down)


def solution(mesh):
    placed = (
        P("col", "row"),
        P("col", "row"),
        P("col"),
        P(),
        P("row", "col"),
        P("row", "col"),
        P("col", "row"),
    )
    return jax.shard_map(
        local,
        mesh=mesh,
        in_specs=placed,
        out_specs=(P("col", "row"), P("row", "col"), P("row", "col"), P("col", "row")),
        check_vma=False,
    )
```

profile of v0, /device:TPU:1, one launch (start us, length us, event | category | flops | bytes accessed | tf_op | source)
XLA Modules:
  0.0 400.2 jit_solution(3114722287939232670)
XLA Ops:
  7.2 0.0 copy-start
  7.2 0.0 reduce-scatter.3.cloned.1.call-start
  7.2 1.0 fusion.2
  8.2 0.8 multiply_convert_fusion.3
  9.1 43.5 %all_gather.16 = bf16[512,512]{1,0:T(8,128)(2,1)S(1)} all-gather(bf16[32,512]{1,0:T(8,128)(2,1)S(1)} %multiply_convert_fusion.3), channel_id=1, replica_groups=mesh['row'=16,'col'=16] {'col'}, dimensions={0}, use_global_device_ids=true | all-gather | bytes 557056 | tf_op jit(solution)/shard_map/all_gather | solution.py:35
  52.5 35.7 %all_gather.15 = bf16[512,512]{1,0:T(8,128)(2,1)S(1)} all-gather(bf16[32,512]{1,0:T(8,128)(2,1)} %param.7), channel_id=1, replica_groups=mesh['row'=16,'col'=16] {'col'}, dimensions={0}, use_global_device_ids=true | all-gather | bytes 557056 | tf_op jit(solution)/shard_map/all_gather | solution.py:34
  88.2 2.6 fusion.6
  90.9 0.0 copy-done
  90.9 0.0 copy-start.1
  90.9 1.1 fusion.5
  92.0 0.4 copy-done.1
  92.4 1.1 fusion.7
  93.5 4.5 %pad_maximum_fusion = f32[512,5376]{1,0:T(8,128)} fusion(f32[512,1792]{1,0:T(8,128)S(1)} %fusion.7, f32[512,1792]{1,0:T(8,128)S(1)} %fusion.6, f32[512,1792]{1,0:T(8,128)S(1)} %fusion.5), kind=kLoop, calls=%fused_computation | loop fusion | flops 5505024 | bytes 22020096 | tf_op jit(solution)/shard_map/concatenate | solution.py:42
  98.0 0.0 reduce-scatter.3.cloned.1.call-update
  98.1 0.0 all-gather.4.cloned.1.call-start
  98.1 89.2 %reduce-scatter.3.cloned.1.call-done = f32[32,5376]{1,0:T(8,128)} async-done(((f32[512,5376]{1,0:T(8,128)}), f32[32,5376]{1,0:T(8,128)}) %reduce-scatter.3.cloned.1.call-update) | async-done | bytes 688144 | tf_op jit(solution)/shard_map/reduce_scatter | solution.py:41
  187.3 2.0 multiply_convert_fusion
  189.3 0.0 all-gather.4.cloned.1.call-update
  189.3 0.0 all-gather.6.cloned.1.call-start
  189.4 0.7 all-gather.6.cloned.1.call-update
  190.1 0.0 all-gather.8.cloned.1.call-start
  190.1 0.5 all-gather.8.cloned.1.call-update
  190.6 0.0 reduce-scatter.5.cloned.1.call-start
  190.7 37.4 %all-gather.4.cloned.1.call-done = bf16[512,1792]{1,0:T(8,128)(2,1)} async-done(((bf16[32,1792]{1,0:T(8,128)(2,1)}), bf16[512,1792]{1,0:T(8,128)(2,1)}) %all-gather.4.cloned.1.call-update) | async-done | bytes 1835024 | tf_op jit(solution)/shard_map/all_gather | solution.py:52
  228.1 3.6 fusion.8
  231.7 35.0 %all-gather.6.cloned.1.call-done = bf16[512,1792]{1,0:T(8,128)(2,1)} async-done(((bf16[32,1792]{1,0:T(8,128)(2,1)}), bf16[512,1792]{1,0:T(8,128)(2,1)}) %all-gather.6.cloned.1.call-update) | async-done | bytes 1835024 | tf_op jit(solution)/shard_map/all_gather | solution.py:53
  266.7 4.4 %convolution_add_fusion = f32[512,512]{1,0:T(8,128)} fusion(f32[512,512]{1,0:T(8,128)} %fusion.8, bf16[512,1792]{1,0:T(8,128)(2,1)} %all-gather.6.cloned.1.call-done, bf16[512,1792]{1,0:T(8,128)(2,1)} %param.12), kind=kOutput, calls=%fused_computation.6 | convolution fusion | flops 939786240 | bytes 5767168 | tf_op jit(solution)/shard_map/dot_general | solution.py:23
  271.2 0.0 reduce-scatter.5.cloned.1.call-update
  271.2 3.9 fusion
  275.1 3.8 copy.11
  278.9 3.9 fusion.1
  282.8 3.8 copy.12
  286.6 18.0 %all-gather.8.cloned.1.call-done = bf16[512,1792]{1,0:T(8,128)(2,1)} async-done(((bf16[32,1792]{1,0:T(8,128)(2,1)}), bf16[512,1792]{1,0:T(8,128)(2,1)}) %all-gather.8.cloned.1.call-update) | async-done | bytes 1835024 | tf_op jit(solution)/shard_map/all_gather | solution.py:51
  304.7 3.9 convolution_convert_fusion
  308.5 83.7 %reduce-scatter.5.cloned.1.call-done = f32[32,512]{1,0:T(8,128)} async-done(((f32[512,512]{1,0:T(8,128)}), f32[32,512]{1,0:T(8,128)}) %reduce-scatter.5.cloned.1.call-update) | async-done | bytes 65552 | tf_op jit(solution)/shard_map/reduce_scatter | solution.py:58
  392.2 1.5 convert_element_type.42
Async XLA Ops:
  7.2 83.7 %copy-start = (bf16[512,1792]{1,0:T(8,128)(2,1)S(1)}, bf16[512,1792]{1,0:T(8,128)(2,1)}, u32[]{:S(2)}) copy-start(bf16[512,1792]{1,0:T(8,128)(2,1)} %param.11) | copy-start | bytes 5505028
  7.2 180.1 %reduce-scatter.3.cloned.1.call-start = ((), (), s32[]{:S(2)}) async-start(), calls=%async_computation.2 | async-start | bytes 11698176 | tf_op jit(solution)/shard_map/reduce_scatter | solution.py:41
  90.9 1.5 copy-start.1
  98.1 130.0 %all-gather.4.cloned.1.call-start = ((), (), s32[]{:S(2)}) async-start(), calls=%async_computation.3 | async-start | bytes 1949696 | tf_op jit(solution)/shard_map/all_gather | solution.py:52
  189.3 77.4 %all-gather.6.cloned.1.call-start = ((), (), s32[]{:S(2)}) async-start(), calls=%async_computation.4 | async-start | bytes 1949696 | tf_op jit(solution)/shard_map/all_gather | solution.py:53
  190.1 114.6 %all-gather.8.cloned.1.call-start = ((), (), s32[]{:S(2)}) async-start(), calls=%async_computation.6 | async-start | bytes 1949696 | tf_op jit(solution)/shard_map/all_gather | solution.py:51
  190.6 201.6 %reduce-scatter.5.cloned.1.call-start = ((), (), s32[]{:S(2)}) async-start(), calls=%async_computation.5 | async-start | bytes 1114112 | tf_op jit(solution)/shard_map/reduce_scatter | solution.py:58
Sparse Core Ops, SparseCore 0:
  98.2 89.0 reduce-scatter.2
  189.7 38.3 all-gather.3
  230.5 36.1 all-gather.5
  268.4 36.1 all-gather.7
  308.0 84.1 reduce-scatter.4
where the time goes:
time: 402 us; the launch traced here: 400 us
  waiting for transfers between devices  265 us (66%)
  blocking collectives  79.2 us (20%)
  matrix products  25.6 us (6%)
  between operations  13.8 us (3%)
  other arithmetic  8.8 us (2%)
  local copies, waits for them, and re-layouts  7.97 us (2%)
    reduce_scatter x1, waiting for transfers between devices, local(): lax.psum_scatter(jnp.concatenate([gate_part, up_part, hidden_part], axis=...  89.2 us
    reduce_scatter x1, waiting for transfers between devices, local(): lax.psum_scatter(contract_cols(grad_pre_gate, gate_weight) + contract_col...  83.7 us
    all_gather x1, blocking collectives, local(): lax.all_gather(weighted, 'col', axis=0, tiled=True)  43.5 us
    all_gather x1, waiting for transfers between devices, local(): lax.all_gather(grad_pre_gate, 'row', axis=0, tiled=True)  37.4 us
    all_gather x1, blocking collectives, local(): lax.all_gather(tokens, 'col', axis=0, tiled=True)  35.7 us
    all_gather x1, waiting for transfers between devices, local(): lax.all_gather(grad_pre_up, 'row', axis=0, tiled=True)  35 us
    all_gather x1, waiting for transfers between devices, local(): lax.all_gather(hidden, 'row', axis=0, tiled=True)  18 us
    dot_general x3, matrix products, contract_rows(): lax.dot_general(left, right, (((0,), (0,)), ((), ())), preferred_element_...  11.7 us
  transfers between devices with their start and end apart: 5, of which 5 were waited for; matrix products, arithmetic and copies ran while one was open for 7% of the time, Pallas kernels for 0%

commit v1 on v0

v1 whole, which is shorter than its diff:
```python
import functools

import jax
import jax.numpy as jnp
from jax import lax
from jax.experimental import pallas as pl
from jax.experimental.pallas import tpu as pltpu
from jax.sharding import PartitionSpec as P

MESH = pl.DeviceIdType.MESH
BF16, F32 = jnp.bfloat16, jnp.float32
NX, NZ, NH, NY = 4, 2, 4, 4
ORDER = (0, 1, 3, 2)
CHUNKS = 4
GX = 9


def contract_last(left, right):
    return lax.dot_general(left, right, (((1,), (1,)), ((), ())), preferred_element_type=F32)


def contract_first(left, right):
    return lax.dot_general(left, right, (((0,), (0,)), ((), ())), preferred_element_type=F32)


def main_kernel(
    seq_ref, conf_ref, tok_ref, og_ref, gate_hbm, up_hbm, down_hbm,
    gtok_ref, h_hbm, a_hbm,
    acts, wg, wu, wd, wg2, wu2,
    part, rx1, rz1, rx2, rz2, own, sx2, sz2, tot, hb, hs,
    gt, sd, rd, se, re, st,
    lsem, wsend, wrecv, asend, arecv, ysend, yrecv, csend, crecv,
    x1s, x1r, z1s, z1r, x2s, x2r, z2s, z2r,
    ax1s, ax1r, az1s, az1r, ax2s, ax2r, az2s, az2r,
    hss, hsr, ds_, dr_, es_, er_,
):
    row, col = lax.axis_index("row"), lax.axis_index("col")
    z, x, c = row // 8, (row // 2) % 4, row % 2
    zh, y = col // 4, col % 4
    sib = 1 - c
    width = wg.shape[2]
    groups = width // 128
    total = 3 * groups

    def dev(x=x, z=z, c=c, zh=zh, y=y):
        return (z * 8 + x * 2 + c, zh * 4 + y)

    def xpeer(i):
        return dev(x=(x + i) % NX)

    def ypeer(i):
        return dev(y=(y + i) % NY)

    def hpeer(i):
        return dev(zh=(zh + i) % NH)

    zpeer, speer = dev(z=1 - z), dev(c=sib)

    def remote(src, dst, ssem, rsem, peer):
        return pltpu.make_async_remote_copy(
            src_ref=src, dst_ref=dst, send_sem=ssem, recv_sem=rsem,
            device_id=peer, device_id_type=MESH,
        )

    sent = []

    def start(copy):
        copy.start()
        sent.append(copy)
        return copy

    bar = pltpu.get_barrier_semaphore()
    peers = [xpeer(i) for i in (1, 2, 3)] + [ypeer(i) for i in (1, 2, 3)]
    peers += [hpeer(i) for i in (1, 2, 3)] + [zpeer, speer]
    for peer in peers:
        pl.semaphore_signal(bar, inc=1, device_id=peer, device_id_type=MESH)

    mine = pl.ds(pl.multiple_of(c * width, 128), width)
    theirs = pl.ds(pl.multiple_of(sib * width, 128), width)
    loads = [
        pltpu.make_async_copy(gate_hbm.at[:, mine], wg.at[c], lsem.at[0]),
        pltpu.make_async_copy(up_hbm.at[:, mine], wu.at[c], lsem.at[1]),
        pltpu.make_async_copy(down_hbm.at[mine, :], wd.at[c], lsem.at[2]),
        pltpu.make_async_copy(gate_hbm.at[:, theirs], wg2, lsem.at[3]),
        pltpu.make_async_copy(up_hbm.at[:, theirs], wu2, lsem.at[4]),
    ]
    for copy in loads:
        copy.start()

    rows = tok_ref.shape[0]
    at = lax.broadcasted_iota(jnp.int32, (rows, 1), 0)
    factor = jnp.zeros((rows, 1), F32)
    for i in range(rows):
        factor = jnp.where(at == i, conf_ref[seq_ref[i]].astype(F32) * 0.25, factor)
    here = pl.ds(pl.multiple_of(zh * rows, rows), rows)
    acts[c, y, 0, here, :] = tok_ref[...]
    acts[c, y, 1, here, :] = (og_ref[...].astype(F32) * factor).astype(BF16)

    pl.semaphore_wait(bar, len(peers))

    block = acts.at[c, y, :, here, :]
    gather = [
        start(remote(block, block, asend.at[i - 1], arecv.at[i - 1], hpeer(i))) for i in (1, 3, 2)
    ]
    weights = [
        start(remote(gate_hbm.at[:, theirs], wg.at[c], wsend.at[0], wrecv.at[0], speer)),
        start(remote(up_hbm.at[:, theirs], wu.at[c], wsend.at[1], wrecv.at[1], speer)),
        start(remote(down_hbm.at[theirs, :], wd.at[c], wsend.at[2], wrecv.at[2], speer)),
    ]
    for copy in gather:
        copy.wait_recv()
    plane = acts.at[c, y]
    cross = {0: start(remote(plane, plane, csend.at[0], crecv.at[0], speer))}
    gather_y = {
        i: start(remote(plane, plane, ysend.at[i - 1], yrecv.at[i - 1], ypeer(i))) for i in (1, 3, 2)
    }
    keep = []

    def forward(k):
        chunk = (y + ORDER[k]) % NY
        if k == 0:
            for copy in loads:
                copy.wait()
        cross[k].wait_recv()
        if k == 0:
            for copy in weights:
                copy.wait_recv()

        def put(first, value):
            for g in range(groups):
                part[k, :, :, first + g] = (
                    value[:, g * 128 : (g + 1) * 128].astype(BF16).reshape(NX, NZ, 16, 128)
                )

        t0, t1 = acts[0, chunk, 0], acts[1, chunk, 0]
        put(0, jnp.dot(t0, wg[0], preferred_element_type=F32)
            + jnp.dot(t1, wg[1], preferred_element_type=F32))
        put(groups, jnp.dot(t0, wu[0], preferred_element_type=F32)
            + jnp.dot(t1, wu[1], preferred_element_type=F32))
        step = {}
        for i in (1, 3, 2):
            step["x", i] = start(remote(
                part.at[k, (x + i) % NX, :, pl.ds(0, GX)], rx1.at[k, i - 1],
                x1s.at[k, i - 1], x1r.at[k, i - 1], xpeer(i)))
        put(2 * groups, contract_last(acts[0, chunk, 1], wd[0])
            + contract_last(acts[1, chunk, 1], wd[1]))
        step["z"] = start(remote(
            part.at[k, :, 1 - z, pl.ds(GX, total - GX)], rz1.at[k], z1s.at[k], z1r.at[k], zpeer))
        return step

    def second(k, step):
        after = {}
        step["z"].wait_recv()
        for i in (0, 1, 2, 3):
            dest = (x + i) % NX
            value = part[k, dest, z, GX:].astype(F32) + rz1[k, dest].astype(F32)
            if i == 0:
                own[k, GX:] = value
            else:
                sz2[k, i - 1] = value.astype(BF16)
                after["x", i] = start(remote(
                    sz2.at[k, i - 1], rz2.at[k, i - 1], z2s.at[k, i - 1], z2r.at[k, i - 1], xpeer(i)))
        for i in (1, 3, 2):
            step["x", i].wait_recv()

        def summed(zz):
            value = part[k, x, zz, :GX].astype(F32)
            for i in range(3):
                value = value + rx1[k, i, zz].astype(F32)
            return value

        sx2[k] = summed(1 - z).astype(BF16)
        after["z"] = start(remote(sx2.at[k], rx2.at[k], x2s.at[k], x2r.at[k], zpeer))
        own[k, :GX] = summed(z)
        return after

    def pointwise(k, step):
        step["z"].wait_recv()
        tot[:GX] = own[k, :GX] + rx2[k].astype(F32)
        for i in (1, 3, 2):
            step["x", i].wait_recv()
        value = own[k, GX:]
        for i in range(3):
            value = value + rz2[k, i].astype(F32)
        tot[GX:] = value
        gate, up, gh = tot[:groups], tot[groups : 2 * groups], tot[2 * groups :]
        sig = 1.0 / (1.0 + jnp.exp(-gate))
        silu = gate * sig
        hb[k, x, z, :groups] = (silu * up).astype(BF16)
        hb[k, x, z, groups : 2 * groups] = (gh * up * sig * (1.0 + gate * (1.0 - sig))).astype(BF16)
        hb[k, x, z, 2 * groups :] = (gh * silu).astype(BF16)
        after = {}
        head, tail = hb.at[k, x, z, pl.ds(0, GX)], hb.at[k, x, z, pl.ds(GX, total - GX)]
        after["z"] = start(remote(head, head, az1s.at[k], az1r.at[k], zpeer))
        for i in (1, 3, 2):
            after["x", i] = start(
                remote(tail, tail, ax1s.at[k, i - 1], ax1r.at[k, i - 1], xpeer(i)))
        return after

    def spread(k, step):
        after = {}
        step["z"].wait_recv()
        head = hb.at[k, x, :, pl.ds(0, GX)]
        for i in (1, 3, 2):
            after["x", i] = start(
                remote(head, head, ax2s.at[k, i - 1], ax2r.at[k, i - 1], xpeer(i)))
        for i in (1, 3, 2):
            step["x", i].wait_recv()
        tail = hb.at[k, :, z, pl.ds(GX, total - GX)]
        after["z"] = start(remote(tail, tail, az2s.at[k], az2r.at[k], zpeer))
        return after

    def share(k, step):
        for i in (1, 3, 2):
            step["x", i].wait_recv()
        step["z"].wait_recv()
        chunk = (y + ORDER[k]) % NY
        copy = pltpu.make_async_copy(hb.at[k], h_hbm.at[c, chunk], lsem.at[5 + 2 * k])
        copy.start()
        keep.append(copy)
        return start(remote(hb.at[k], hs.at[k], hss.at[k], hsr.at[k], speer))

    def backward(k, copy):
        def flat(ref, first):
            return jnp.concatenate(
                [ref[k, :, :, first + g].reshape(NX * NZ * 16, 128) for g in range(groups)], axis=1)

        value = contract_last(flat(hb, groups), wg[c]) + contract_last(flat(hb, 2 * groups), wu[c])
        copy.wait_recv()
        chunk = (y + ORDER[k]) % NY
        out = pltpu.make_async_copy(hs.at[k], h_hbm.at[sib, chunk], lsem.at[6 + 2 * k])
        out.start()
        keep.append(out)
        value = value + contract_last(flat(hs, groups), wg2[...]) + contract_last(flat(hs, 2 * groups), wu2[...])
        i = ORDER[k]
        if i == 0:
            gt[...] = value
            return None
        sd[i - 1] = value.astype(BF16)
        return start(remote(sd.at[i - 1], rd.at[i - 1], ds_.at[i - 1], dr_.at[i - 1], ypeer(i)))

    def take(k):
        i = (NY - ORDER[k]) % NY
        gather_y[i].wait_recv()
        got = acts.at[c, (y + ORDER[k]) % NY]
        cross[k] = start(remote(got, got, csend.at[k], crecv.at[k], speer))

    s1, s2, s3, s4, s5, s6 = {}, {}, {}, {}, {}, {}
    s1[0] = forward(0)
    take(1)
    take(2)
    s1[1] = forward(1)
    s2[0] = second(0, s1[0])
    s3[0] = pointwise(0, s2[0])
    s1[2] = forward(2)
    take(3)
    s2[1] = second(1, s1[1])
    s4[0] = spread(0, s3[0])
    s3[1] = pointwise(1, s2[1])
    s5[0] = share(0, s4[0])
    s1[3] = forward(3)
    s2[2] = second(2, s1[2])
    s4[1] = spread(1, s3[1])
    s6[0] = backward(0, s5[0])
    s3[2] = pointwise(2, s2[2])
    s5[1] = share(1, s4[1])
    s2[3] = second(3, s1[3])
    s4[2] = spread(2, s3[2])
    s6[1] = backward(1, s5[1])
    s3[3] = pointwise(3, s2[3])
    s5[2] = share(2, s4[2])
    s4[3] = spread(3, s3[3])
    s6[2] = backward(2, s5[2])
    s5[3] = share(3, s4[3])
    s6[3] = backward(3, s5[3])
    out = pltpu.make_async_copy(acts.at[c], a_hbm, lsem.at[13])
    out.start()
    keep.append(out)

    for k in range(1, CHUNKS):
        s6[k].wait_recv()
    value = gt[...]
    for i in range(3):
        value = value + rd[i].astype(F32)
    st[...] = value
    last = {}
    for i in (2, 1, 3):
        there = pl.ds(pl.multiple_of(((zh + i) % NH) * rows, rows), rows)
        se[i - 1] = st[there, :].astype(BF16)
        last[i] = start(remote(se.at[i - 1], re.at[i - 1], es_.at[i - 1], er_.at[i - 1], hpeer(i)))
    value = st[here, :]
    for i in (1, 3, 2):
        last[i].wait_recv()
        value = value + re[i - 1].astype(F32)
    gtok_ref[...] = value.astype(BF16)
    for copy in sent:
        copy.wait_send()
    for copy in keep:
        copy.wait()


def grads_kernel(a_hbm, h_hbm, gg_hbm, gu_hbm, gd_hbm, acts, h, og, ou, od, lsem, osem):
    chunks, _, _, total = h_hbm.shape[1:5]
    groups = total // 3
    width = groups * 128
    loads = [pltpu.make_async_copy(a_hbm, acts, lsem.at[0])]
    loads[0].start()
    order = [(half, which) for half in range(2) for which in (1, 2, 0)]
    for n, (half, which) in enumerate(order):
        span = pl.ds(which * groups, groups)
        copy = pltpu.make_async_copy(
            h_hbm.at[half, :, :, :, span], h.at[half, :, :, :, span], lsem.at[n + 1])
        copy.start()
        loads.append(copy)
    loads[0].wait()
    tokens, depth = chunks * acts.shape[2], acts.shape[3]
    stores = []
    for n, (half, which) in enumerate(order):
        loads[n + 1].wait()
        right = jnp.concatenate(
            [h[half, :, :, :, which * groups + g].reshape(tokens, 128) for g in range(groups)], axis=1)
        left = acts[:, 1 if which == 0 else 0].reshape(tokens, depth)
        span = pl.ds(half * width, width)
        if which == 0:
            od[span, :] = contract_first(right, left).astype(BF16)
            copy = pltpu.make_async_copy(od.at[span, :], gd_hbm.at[span, :], osem.at[n])
        else:
            ref, hbm = ((og, gg_hbm), (ou, gu_hbm))[which - 1]
            ref[:, span] = contract_first(left, right).astype(BF16)
            copy = pltpu.make_async_copy(ref.at[:, span], hbm.at[:, span], osem.at[n])
        copy.start()
        stores.append(copy)
    for copy in stores:
        copy.wait()


def local(tokens, out_grad, seq_ids, confidence, gate_weight, up_weight, down_weight):
    rows, depth = tokens.shape
    width = gate_weight.shape[1] // 2
    groups = width // 128
    total = 3 * groups
    gz = total - GX
    chunk = rows * NH
    vm, dma = pltpu.VMEM, pltpu.SemaphoreType.DMA
    anyspace = pl.BlockSpec(memory_space=pl.ANY)
    vmspace = pl.BlockSpec(memory_space=pltpu.VMEM)
    smspace = pl.BlockSpec(memory_space=pltpu.SMEM)
    four, three = (CHUNKS,), (CHUNKS, 3)
    grad_tokens, h, acts = pl.pallas_call(
        main_kernel,
        name="exchange",
        out_shape=(
            jax.ShapeDtypeStruct((rows, depth), BF16),
            jax.ShapeDtypeStruct((2, NY, NX, NZ, total, 16, 128), BF16),
            jax.ShapeDtypeStruct((NY, 2, chunk, depth), BF16),
        ),
        in_specs=[smspace, smspace, vmspace, vmspace, anyspace, anyspace, anyspace],
        out_specs=(vmspace, anyspace, anyspace),
        scratch_shapes=[
            vm((2, NY, 2, chunk, depth), BF16),
            vm((2, depth, width), BF16),
            vm((2, depth, width), BF16),
            vm((2, width, depth), BF16),
            vm((depth, width), BF16),
            vm((depth, width), BF16),
            vm((CHUNKS, NX, NZ, total, 16, 128), BF16),
            vm((CHUNKS, 3, NZ, GX, 16, 128), BF16),
            vm((CHUNKS, NX, gz, 16, 128), BF16),
            vm((CHUNKS, GX, 16, 128), BF16),
            vm((CHUNKS, 3, gz, 16, 128), BF16),
            vm((CHUNKS, total, 16, 128), F32),
            vm((CHUNKS, GX, 16, 128), BF16),
            vm((CHUNKS, 3, gz, 16, 128), BF16),
            vm((total, 16, 128), F32),
            vm((CHUNKS, NX, NZ, total, 16, 128), BF16),
            vm((CHUNKS, NX, NZ, total, 16, 128), BF16),
            vm((chunk, depth), F32),
            vm((3, chunk, depth), BF16),
            vm((3, chunk, depth), BF16),
            vm((3, rows, depth), BF16),
            vm((3, rows, depth), BF16),
            vm((chunk, depth), F32),
            dma((14,)), dma((3,)), dma((3,)), dma((3,)), dma((3,)), dma((3,)), dma((3,)),
            dma(four), dma(four),
            dma(three), dma(three), dma(four), dma(four), dma(four), dma(four), dma(three), dma(three),
            dma(three), dma(three), dma(four), dma(four), dma(three), dma(three), dma(four), dma(four),
            dma(four), dma(four), dma((3,)), dma((3,)), dma((3,)), dma((3,)),
        ],
        compiler_params=pltpu.CompilerParams(
            collective_id=0, has_side_effects=True, vmem_limit_bytes=48 << 20),
    )(seq_ids, confidence, tokens, out_grad, gate_weight, up_weight, down_weight)
    grad_gate, grad_up, grad_down = pl.pallas_call(
        grads_kernel,
        name="weight_grads",
        out_shape=(
            jax.ShapeDtypeStruct((depth, 2 * width), BF16),
            jax.ShapeDtypeStruct((depth, 2 * width), BF16),
            jax.ShapeDtypeStruct((2 * width, depth), BF16),
        ),
        in_specs=[anyspace, anyspace],
        out_specs=(anyspace, anyspace, anyspace),
        scratch_shapes=[
            vm((NY, 2, chunk, depth), BF16),
            vm((2, NY, NX, NZ, total, 16, 128), BF16),
            vm((depth, 2 * width), BF16),
            vm((depth, 2 * width), BF16),
            vm((2 * width, depth), BF16),
            dma((7,)),
            dma((6,)),
        ],
        compiler_params=pltpu.CompilerParams(vmem_limit_bytes=48 << 20),
    )(acts, h)
    return grad_tokens, grad_gate, grad_up, grad_down


def solution(mesh):
    placed = (
        P("col", "row"),
        P("col", "row"),
        P("col"),
        P(),
        P("row", "col"),
        P("row", "col"),
        P("col", "row"),
    )
    return jax.shard_map(
        local,
        mesh=mesh,
        in_specs=placed,
        out_specs=(P("col", "row"), P("row", "col"), P("row", "col"), P("col", "row")),
        check_vma=False,
    )
```

time: 402 us -> 108 us (0.27)
  waiting for transfers between devices: 265 us -> 0 us
  Pallas kernels: 0 us -> 101 us
  blocking collectives: 79.2 us -> 0 us
  matrix products: 25.6 us -> 0 us
  between operations: 13.8 us -> 0.66 us
  other arithmetic: 8.8 us -> 0 us
    reduce_scatter x2 -> x0, waiting for transfers between devices: 173 us -> none  [the longest x1 89.2 us: local(): lax.psum_scatter(jnp.concatenate([gate_part, up_part, hidden_part], axis=...]
    pallas_call x0 -> x2, Pallas kernels: none -> 101 us  [the longest x1 94.5 us: local(): pl.pallas_call(main_kernel, name='exchange', out_shape=(jax.ShapeDtypeStr...]
    all_gather x3 -> x0, waiting for transfers between devices: 90.5 us -> none  [the longest x1 37.4 us: local(): lax.all_gather(grad_pre_gate, 'row', axis=0, tiled=True)]
    all_gather x2 -> x0, blocking collectives: 79.2 us -> none  [the longest x1 43.5 us: local(): lax.all_gather(weighted, 'col', axis=0, tiled=True)]
    dot_general x9 -> x0, matrix products: 25.6 us -> none  [the longest x3 11.7 us: contract_rows(): lax.dot_general(left, right, (((0,), (0,)), ((), ())), preferred_element_...]
    concatenate x1 -> x0, other arithmetic: 4.51 us -> none  [local(): jnp.concatenate([gate_part, up_part, hidden_part], axis=1)]
    convert_element_type x3 -> x0, other arithmetic: 4.28 us -> none  [the longest x1 1.99 us: pointwise(): hidden = (silu_gate * up).astype(jnp.bfloat16)]
  transfers between devices with their start and end apart: 5 -> 0, of which waited for: 5 -> 0; matrix products, arithmetic and copies ran while one was open for 7% -> 0% of each run, Pallas kernels for 0% -> 0%
where the time goes in v1:
time: 108 us
  Pallas kernels  101 us (94%)
  local copies, waits for them, and re-layouts  6.43 us (6%)
    pallas_call x1, Pallas kernels, local(): pl.pallas_call(main_kernel, name='exchange', out_shape=(jax.ShapeDtypeStr...  94.5 us
    pallas_call x1, Pallas kernels, local(): pl.pallas_call(grads_kernel, name='weight_grads', out_shape=(jax.ShapeDty...  6.61 us
    unnamed x13, local copies, waits for them, and re-layouts  6.43 us

profile of v1, /device:TPU:1, one launch (start us, length us, event | category | flops | bytes accessed | tf_op | source)
XLA Modules:
  0.0 108.2 jit_solution(1253290372314559809)
XLA Ops:
  0.6 0.0 copy-start
  0.6 1.5 %copy-done = bf16[512,1792]{1,0:T(8,128)(2,1)S(1)} copy-done((bf16[512,1792]{1,0:T(8,128)(2,1)S(1)}, bf16[512,1792]{1,0:T(8,128)(2,1)}, u32[]{:S(2)}) %copy-start) | copy-done | bytes 1835032
  2.1 0.0 copy-start.1
  2.1 1.5 %copy-done.1 = bf16[512,1792]{1,0:T(8,128)(2,1)S(1)} copy-done((bf16[512,1792]{1,0:T(8,128)(2,1)S(1)}, bf16[512,1792]{1,0:T(8,128)(2,1)}, u32[]{:S(2)}) %copy-start.1) | copy-done | bytes 1835032
  3.6 0.0 copy-start.2
  3.6 0.8 copy-done.2
  4.4 0.0 copy-start.3
  4.4 0.8 copy-done.3
  5.2 0.0 copy-start.4
  5.2 0.7 copy-done.4
  5.8 0.0 copy-start.5
  5.8 0.7 copy-done.5
  6.5 94.5 %exchange.1 = (bf16[32,512]{1,0:T(8,128)(2,1)S(1)}, bf16[2,4,4,2,21,16,128]{6,5,4,3,2,1,0:T(8,128)(2,1)}, bf16[4,2,128,512]{3,2,1,0:T(8,128)(2,1)S(1)}) custom-call(s32[32]{0:T(128)S(1)} %copy-done.4, s32[8]{0:T(128)S(1)} %copy-done.5, bf16[32,512]{1,0:T(8,128)(2,1)S(1)} %copy-done.2, bf16[32,512]{1,0:T(8,128)(2,1)S(1)} %copy-done.3, ...), custom_call_target="tpu_custom_call" | custom-call | tf_op jit(solution)/shard_map/exchange/pallas_call | solution.py:349
  101.0 6.6 %weight_grads.1 = (bf16[512,1792]{1,0:T(8,128)(2,1)}, bf16[512,1792]{1,0:T(8,128)(2,1)}, bf16[1792,512]{1,0:T(8,128)(2,1)}) custom-call(bf16[4,2,128,512]{3,2,1,0:T(8,128)(2,1)S(1)} %get-tuple-element.11.a_hbm, bf16[2,4,4,2,21,16,128]{6,5,4,3,2,1,0:T(8,128)(2,1)} %get-tuple-element.12.h_hbm), custom_call_target="tpu_custom_call" | custom-call | tf_op jit(solution)/shard_map/weight_grads/pallas_call | solution.py:392
  107.6 0.6 copy.12
Async XLA Ops:
  0.6 1.5 %copy-start = (bf16[512,1792]{1,0:T(8,128)(2,1)S(1)}, bf16[512,1792]{1,0:T(8,128)(2,1)}, u32[]{:S(2)}) copy-start(bf16[512,1792]{1,0:T(8,128)(2,1)} %gate_hbm.1) | copy-start | bytes 5505028
  2.1 1.5 %copy-start.1 = (bf16[512,1792]{1,0:T(8,128)(2,1)S(1)}, bf16[512,1792]{1,0:T(8,128)(2,1)}, u32[]{:S(2)}) copy-start(bf16[512,1792]{1,0:T(8,128)(2,1)} %up_hbm.1) | copy-start | bytes 5505028
  3.6 0.8 copy-start.2
  4.4 0.8 copy-start.3
  5.2 0.7 copy-start.4
  5.8 0.7 copy-start.5

commit v2 on v0

v2 whole, which is shorter than its diff:
```python
import jax
import jax.numpy as jnp
from jax import lax
from jax.experimental import pallas as pl
from jax.experimental.pallas import tpu as pltpu
from jax.sharding import PartitionSpec as P

MESH = pl.DeviceIdType.MESH
BF16, F32 = jnp.bfloat16, jnp.float32
NX, NZ, NH, NY = 4, 2, 4, 4
CHUNKS = 4
ORDER = (0, 1, 3, 2)
NA = 5
SCHEDULE = (
    "T0", "Z2", "FA0", "FB0", "Z1", "Z3", "MA0", "T2", "SB0", "FA2", "FB2", "T1", "SA0", "MB0", "FA1", "FB1",
    "T3", "MA2", "SB2", "FA3", "PB0", "FB3", "PA0", "MA1", "SB1", "SA2", "MB2", "SB3", "MA3", "AA0", "WB0",
    "PA2", "SA1", "MB1", "PB2", "MB3", "SA3", "AA2", "PA1", "WA0", "YB0", "PB1", "WB2", "PA3", "PB3", "AA1",
    "WA2", "HB0", "HA0", "BA0", "BB0", "YB2", "WB1", "AA3", "WB3", "C0", "WA1", "HB2", "HA2", "BA2", "BB2",
    "YB1", "D0", "C2", "WA3", "YB3", "HA1", "BA1", "HB1", "BB1", "HA3", "BA3", "D2", "C1", "HB3", "BB3",
    "G0", "G1", "C3", "G2", "G3", "G4", "D1", "G5", "D3", "E0",
)

def contract_last(left, right):
    return lax.dot_general(left, right, (((1,), (1,)), ((), ())), preferred_element_type=F32)


def contract_first(left, right):
    return lax.dot_general(left, right, (((0,), (0,)), ((), ())), preferred_element_type=F32)


def pointwise(gate, up, gh):
    sig = 1.0 / (1.0 + jnp.exp(-gate))
    silu = gate * sig
    hidden = (silu * up).astype(BF16)
    grad_pre_gate = (gh * up * sig * (1.0 + gate * (1.0 - sig))).astype(BF16)
    grad_pre_up = (gh * silu).astype(BF16)
    return hidden, grad_pre_gate, grad_pre_up


def main_kernel(
    seq_hbm, conf_hbm, tok_hbm, grad_hbm, gate_hbm, up_hbm, down_hbm,
    gtok_ref, gg_hbm, gu_hbm, gd_hbm,
    seq, conf, raw, acts, wg, wu, wd, part, full,
    far_a, fin_a, sum_a, mid_a, out_a, in_a, own_a,
    in_b, full_b, part_b, far_b, fin_b, sum_b, mid_b,
    tot, hb, hs, gp, gq, gr, sd, rd, se, re, own_t, og, ou, od,
    lsem, osem, wsem, hsem, ysem, csem,
    far_as, fin_as, sum_as, z_as, gz_as, gx_as, gw_as, sh_as,
    far_bs, fin_bs, sum_bs, z_bs, gz_bs, gx_bs, gw_bs, sh_bs,
    psem, dsem, esem,
):
    row, col = lax.axis_index("row"), lax.axis_index("col")
    z, x, c = row // 8, (row // 2) % 4, row % 2
    zh, y = col // 4, col % 4
    sib = 1 - c
    width = wg.shape[2]
    groups = width // 128
    nb = groups - NA
    ga, gb = 3 * NA, 3 * nb
    rows = raw.shape[0]
    right, left = (x + 1) % NX, (x + 3) % NX
    across = (x + 2) % NX

    def dev(x=x, z=z, c=c, zh=zh, y=y):
        return (z * 8 + x * 2 + c, zh * 4 + y)

    def ypeer(i):
        return dev(y=(y + i) % NY)

    def hpeer(i):
        return dev(zh=(zh + i) % NH)

    zpeer, speer = dev(z=1 - z), dev(c=sib)
    xpeers = (dev(x=right), dev(x=left))

    sent, kept, state = [], [], {}

    def send(key, src, dst, sems, index, peer):
        copy = pltpu.make_async_remote_copy(
            src_ref=src, dst_ref=dst, send_sem=sems.at[(0,) + index], recv_sem=sems.at[(1,) + index],
            device_id=peer, device_id_type=MESH)
        copy.start()
        sent.append(copy)
        state[key] = copy

    def wait(key):
        state[key].wait_recv()

    def local(src, dst, sem):
        copy = pltpu.make_async_copy(src, dst, sem)
        copy.start()
        return copy

    bar = pltpu.get_barrier_semaphore()
    peers = list(xpeers) + [ypeer(i) for i in (1, 2, 3)] + [hpeer(i) for i in (1, 2, 3)] + [zpeer, speer]
    for peer in peers:
        pl.semaphore_signal(bar, inc=1, device_id=peer, device_id_type=MESH)

    def yrows(i):
        return pl.ds(pl.multiple_of(((y + i) % NY) * rows, rows), rows)

    first = [
        local(seq_hbm, seq, lsem.at[0]),
        local(conf_hbm, conf, lsem.at[1]),
        local(grad_hbm, raw, lsem.at[2]),
        local(tok_hbm, acts.at[c, zh, 0, yrows(0), :], lsem.at[3]),
    ]
    mine = pl.ds(pl.multiple_of(c * width, 128), width)
    theirs = pl.ds(pl.multiple_of(sib * width, 128), width)
    loads = [
        local(gate_hbm.at[:, mine], wg.at[c], lsem.at[4]),
        local(up_hbm.at[:, mine], wu.at[c], lsem.at[5]),
        local(down_hbm.at[mine, :], wd.at[c], lsem.at[6]),
    ]
    for copy in first:
        copy.wait()
    at = lax.broadcasted_iota(jnp.int32, (rows, 1), 0)
    factor = jnp.zeros((rows, 1), F32)
    for i in range(rows):
        factor = jnp.where(at == i, conf[seq[i]].astype(F32) * 0.25, factor)
    acts[c, zh, 1, yrows(0), :] = (raw[...].astype(F32) * factor).astype(BF16)
    pl.semaphore_wait(bar, len(peers))

    def plane(k):
        return (zh + ORDER[k]) % NH

    def to_y(k):
        block = acts.at[c, plane(k), :, yrows(0), :]
        for i in (1, 3, 2):
            send(("y", k, i), block, block, ysem, (k, i - 1), ypeer(i))

    to_y(0)
    block = acts.at[c, zh, :, yrows(0), :]
    for i in (1, 3, 2):
        send(("h", i), block, block, hsem, (i - 1,), hpeer(i))
    send(("w", 0), gate_hbm.at[:, theirs], wg.at[c], wsem, (0,), speer)
    send(("w", 1), up_hbm.at[:, theirs], wu.at[c], wsem, (1,), speer)
    send(("w", 2), down_hbm.at[theirs, :], wd.at[c], wsem, (2,), speer)

    def pass_y(k):
        wait(("h", (NH - ORDER[k]) % NH))
        to_y(k)

    def take(k):
        for i in (1, 3, 2):
            wait(("y", k, i))
        got = acts.at[c, plane(k)]
        send(("c", k), got, got, csem, (k,), speer)

    def product(k, which, lo, n):
        span = pl.ds(lo * 128, n * 128)
        arr = 1 if which == 2 else 0
        t0, t1 = acts[0, plane(k), arr], acts[1, plane(k), arr]
        if which == 2:
            value = contract_last(t0, wd[0, span, :]) + contract_last(t1, wd[1, span, :])
        else:
            w = (wg, wu)[which]
            value = jnp.dot(t0, w[0, :, span], preferred_element_type=F32) + jnp.dot(
                t1, w[1, :, span], preferred_element_type=F32)
        base = which * NA if lo == 0 else ga + which * nb
        for g in range(n):
            v = value[:, g * 128 : (g + 1) * 128].reshape(NX, NZ, 16, 128)
            full[k, :, :, base + g] = v
            part[k, :, :, base + g] = v.astype(BF16)

    def halves(n, k):
        cut = (n + 1 - k % 2) // 2
        return (0, cut), (cut, n - cut)

    def forward_a(k):
        if k == 0:
            for copy in loads:
                copy.wait()
        wait(("c", k))
        for which in range(3):
            if k == 0:
                wait(("w", which))
            product(k, which, 0, NA)
        for d in range(2):
            lo, n = halves(ga, k)[d]
            send(("far_a", k, d), part.at[k, across, :, pl.ds(lo, n)], far_a.at[k, d, :, pl.ds(0, n)],
                 far_as, (k, d), xpeers[d])
        for d in range(2):
            lo, n = halves(ga, k)[1 - d]
            send(("fin_a", k, d), part.at[k, (right, left)[d], :, pl.ds(lo, n)],
                 fin_a.at[k, d, :, pl.ds(0, n)], fin_as, (k, d), xpeers[d])

    def middle_a(k):
        for d in range(2):
            lo, n = halves(ga, k)[d]
            wait(("far_a", k, d))
            value = full[k, (right, left)[d], :, lo : lo + n] + far_a[k, d, :, :n].astype(F32)
            mid_a[k, d, :, :n] = value.astype(BF16)
            span = pl.ds(0, n)
            send(("sum_a", k, d), mid_a.at[k, d, :, span], sum_a.at[k, d, :, span],
                 sum_as, (k, d), xpeers[d])

    def second_a(k):
        for d in range(2):
            wait(("fin_a", k, d))
        for d in range(2):
            wait(("sum_a", k, d))
        for zz in (1 - z, z):
            for d in range(2):
                lo, n = halves(ga, k)[d]
                value = (full[k, x, zz, lo : lo + n] + sum_a[k, d, zz, :n].astype(F32)
                         + fin_a[k, 1 - d, zz, :n].astype(F32))
                if zz is z:
                    own_a[k, lo : lo + n] = value
                else:
                    out_a[k, lo : lo + n] = value.astype(BF16)
            if zz is not z:
                send(("z_a", k), out_a.at[k], in_a.at[k], z_as, (k,), zpeer)

    def point_a(k):
        wait(("z_a", k))
        value = own_a[k] + in_a[k].astype(F32)
        results = pointwise(value[:NA], value[NA : 2 * NA], value[2 * NA :])
        for which in range(3):
            hb[k, x, z, which * NA : (which + 1) * NA] = results[which]
        block = hb.at[k, x, z, pl.ds(0, ga)]
        send(("gz_a", k), block, block, gz_as, (k,), zpeer)

    def across_a(k):
        wait(("gz_a", k))
        block = hb.at[k, x, :, pl.ds(0, ga)]
        for d in range(2):
            send(("gx_a", k, d), block, block, gx_as, (k, d), xpeers[d])

    def onward_a(k):
        for d in range(2):
            lo, n = halves(ga, k)[d]
            wait(("gx_a", k, d))
            block = hb.at[k, (left, right)[d], :, pl.ds(lo, n)]
            send(("gw_a", k, d), block, block, gw_as, (k, d), xpeers[d])

    def share_a(k):
        for d in range(2):
            wait(("gw_a", k, d))
        send(("sh_a", k), hb.at[k, :, :, pl.ds(0, ga)], hs.at[k, :, :, pl.ds(0, ga)], sh_as, (k,), speer)

    def forward_b(k):
        for which in range(3):
            product(k, which, NA, nb)
        send(("z_b", k), part.at[k, :, 1 - z, pl.ds(ga, gb)], in_b.at[k], z_bs, (k,), zpeer)

    def second_b(k):
        wait(("z_b", k))
        value = full[k, :, z, ga:] + in_b[k].astype(F32)
        full_b[k] = value
        part_b[k] = value.astype(BF16)
        for d in range(2):
            lo, n = halves(gb, k)[d]
            send(("far_b", k, d), part_b.at[k, across, pl.ds(lo, n)], far_b.at[k, d, pl.ds(0, n)],
                 far_bs, (k, d), xpeers[d])
        for d in range(2):
            lo, n = halves(gb, k)[1 - d]
            send(("fin_b", k, d), part_b.at[k, (right, left)[d], pl.ds(lo, n)],
                 fin_b.at[k, d, pl.ds(0, n)], fin_bs, (k, d), xpeers[d])

    def middle_b(k):
        for d in range(2):
            lo, n = halves(gb, k)[d]
            wait(("far_b", k, d))
            value = full_b[k, (right, left)[d], lo : lo + n] + far_b[k, d, :n].astype(F32)
            mid_b[k, d, :n] = value.astype(BF16)
            span = pl.ds(0, n)
            send(("sum_b", k, d), mid_b.at[k, d, span], sum_b.at[k, d, span], sum_bs, (k, d), xpeers[d])

    def point_b(k):
        for d in range(2):
            wait(("fin_b", k, d))
        for d in range(2):
            wait(("sum_b", k, d))
        for d in range(2):
            lo, n = halves(gb, k)[d]
            tot[lo : lo + n] = (full_b[k, x, lo : lo + n] + sum_b[k, d, :n].astype(F32)
                                + fin_b[k, 1 - d, :n].astype(F32))
        results = pointwise(tot[:nb], tot[nb : 2 * nb], tot[2 * nb :])
        for which in range(3):
            hb[k, x, z, ga + which * nb : ga + (which + 1) * nb] = results[which]
        block = hb.at[k, x, z, pl.ds(ga, gb)]
        for d in range(2):
            send(("gx_b", k, d), block, block, gx_bs, (k, d), xpeers[d])

    def onward_b(k):
        for d in range(2):
            lo, n = halves(gb, k)[d]
            wait(("gx_b", k, d))
            block = hb.at[k, (left, right)[d], z, pl.ds(ga + lo, n)]
            send(("gw_b", k, d), block, block, gw_bs, (k, d), xpeers[d])

    def across_b(k):
        for d in range(2):
            wait(("gw_b", k, d))
        block = hb.at[k, :, z, pl.ds(ga, gb)]
        send(("gz_b", k), block, block, gz_bs, (k,), zpeer)

    def share_b(k):
        wait(("gz_b", k))
        send(("sh_b", k), hb.at[k, :, :, pl.ds(ga, gb)], hs.at[k, :, :, pl.ds(ga, gb)], sh_bs, (k,), speer)

    def flat(ref, k, first, n):
        return [ref[k, :, :, first + g].reshape(NX * NZ * 16, 128) for g in range(n)]

    def back(k, base, lo, n):
        dg = jnp.concatenate(flat(hb, k, base + n, n), axis=1)
        du = jnp.concatenate(flat(hb, k, base + 2 * n, n), axis=1)
        span = pl.ds(lo * 128, n * 128)
        return [contract_last(dg, wg[h, :, span]) + contract_last(du, wu[h, :, span]) for h in (sib, c)]

    def back_a(k):
        gq[k], gp[k] = back(k, 0, 0, NA)

    def back_b(k):
        other, own = back(k, ga, NA, nb)
        gq[k] = gq[k] + other
        send(("p", k), gq.at[k], gr.at[k], psem, (k,), speer)
        gp[k] = gp[k] + own

    def cols_send(k):
        wait(("p", k))
        gp[k] = gp[k] + gr[k]
        for i in (2, 1, 3):
            sd[k, i - 1] = gp[k, yrows(i), :].astype(BF16)
            send(("d", k, i), sd.at[k, i - 1], rd.at[k, i - 1], dsem, (k, i - 1), ypeer(i))

    def cols_sum(k):
        value = gp[k, yrows(0), :]
        for i in (1, 3, 2):
            wait(("d", k, i))
            value = value + rd[k, i - 1].astype(F32)
        i = ORDER[k]
        if i == 0:
            own_t[...] = value
        else:
            se[i - 1] = value.astype(BF16)
            send(("e", i), se.at[i - 1], re.at[i - 1], esem, (i - 1,), hpeer(i))

    def finish(_):
        value = own_t[...]
        for i in (1, 3, 2):
            wait(("e", i))
            value = value + re[i - 1].astype(F32)
        gtok_ref[...] = value.astype(BF16)

    def weight_grads(n):
        ref, half = (hb, c) if n < 3 else (hs, sib)
        which = (1, 2, 0)[n % 3]
        if n == 3:
            for k in range(CHUNKS):
                wait(("sh_a", k))
                wait(("sh_b", k))
        cols = [jnp.concatenate(v, axis=0) for v in zip(*(
            flat(ref, k, which * NA, NA) + flat(ref, k, ga + which * nb, nb) for k in range(CHUNKS)))]
        units = jnp.concatenate(cols, axis=1)
        acted = jnp.concatenate([acts[c, plane(k), 1 if which == 0 else 0] for k in range(CHUNKS)], axis=0)
        span = pl.ds(pl.multiple_of(half * width, 128), width)
        if which == 0:
            od[span, :] = contract_first(units, acted).astype(BF16)
            kept.append(local(od.at[span, :], gd_hbm.at[span, :], osem.at[n]))
        else:
            out, hbm = ((og, gg_hbm), (ou, gu_hbm))[which - 1]
            out[:, span] = contract_first(acted, units).astype(BF16)
            kept.append(local(out.at[:, span], hbm.at[:, span], osem.at[n]))

    stages = dict(
        Z=pass_y, T=take, FA=forward_a, FB=forward_b, MA=middle_a, SA=second_a, PA=point_a, AA=across_a,
        WA=onward_a, HA=share_a, SB=second_b, MB=middle_b, PB=point_b, WB=onward_b, YB=across_b,
        HB=share_b, BA=back_a, BB=back_b, C=cols_send, D=cols_sum, E=finish, G=weight_grads)
    for item in SCHEDULE:
        stages[item[:-1]](int(item[-1]))
    for copy in sent:
        copy.wait_send()
    for copy in kept:
        copy.wait()


def local(tokens, out_grad, seq_ids, confidence, gate_weight, up_weight, down_weight):
    rows, depth = tokens.shape
    width = gate_weight.shape[1] // 2
    groups = width // 128
    nb = groups - NA
    ga, gb = 3 * NA, 3 * nb
    ha, hb = (ga + 1) // 2, (gb + 1) // 2
    total = ga + gb
    chunk = rows * NY
    k = CHUNKS
    vm, sm, dma = pltpu.VMEM, pltpu.SMEM, pltpu.SemaphoreType.DMA
    anyspace = pl.BlockSpec(memory_space=pl.ANY)
    vmspace = pl.BlockSpec(memory_space=pltpu.VMEM)
    one, two = dma((2, k)), dma((2, k, 2))
    return pl.pallas_call(
        main_kernel,
        name="exchange",
        out_shape=(
            jax.ShapeDtypeStruct((rows, depth), BF16),
            jax.ShapeDtypeStruct((depth, 2 * width), BF16),
            jax.ShapeDtypeStruct((depth, 2 * width), BF16),
            jax.ShapeDtypeStruct((2 * width, depth), BF16),
        ),
        in_specs=[anyspace] * 7,
        out_specs=(vmspace, anyspace, anyspace, anyspace),
        scratch_shapes=[
            sm(seq_ids.shape, jnp.int32),
            sm(confidence.shape, jnp.int32),
            vm((rows, depth), BF16),
            vm((2, NH, 2, chunk, depth), BF16),
            vm((2, depth, width), BF16),
            vm((2, depth, width), BF16),
            vm((2, width, depth), BF16),
            vm((k, NX, NZ, total, 16, 128), BF16),
            vm((k, NX, NZ, total, 16, 128), F32),
            vm((k, 2, NZ, ha, 16, 128), BF16),
            vm((k, 2, NZ, ha, 16, 128), BF16),
            vm((k, 2, NZ, ha, 16, 128), BF16),
            vm((k, 2, NZ, ha, 16, 128), BF16),
            vm((k, ga, 16, 128), BF16),
            vm((k, ga, 16, 128), BF16),
            vm((k, ga, 16, 128), F32),
            vm((k, NX, gb, 16, 128), BF16),
            vm((k, NX, gb, 16, 128), F32),
            vm((k, NX, gb, 16, 128), BF16),
            vm((k, 2, hb, 16, 128), BF16),
            vm((k, 2, hb, 16, 128), BF16),
            vm((k, 2, hb, 16, 128), BF16),
            vm((k, 2, hb, 16, 128), BF16),
            vm((gb, 16, 128), F32),
            vm((k, NX, NZ, total, 16, 128), BF16),
            vm((k, NX, NZ, total, 16, 128), BF16),
            vm((k, chunk, depth), F32),
            vm((k, chunk, depth), F32),
            vm((k, chunk, depth), F32),
            vm((k, 3, rows, depth), BF16),
            vm((k, 3, rows, depth), BF16),
            vm((3, rows, depth), BF16),
            vm((3, rows, depth), BF16),
            vm((rows, depth), F32),
            vm((depth, 2 * width), BF16),
            vm((depth, 2 * width), BF16),
            vm((2 * width, depth), BF16),
            dma((7,)), dma((6,)), dma((2, 3)), dma((2, 3)), dma((2, k, 3)), one,
            two, two, two, one, one, two, two, one,
            two, two, two, one, one, two, two, one,
            one, dma((2, k, 3)), dma((2, 3)),
        ],
        compiler_params=pltpu.CompilerParams(
            collective_id=0, has_side_effects=True, vmem_limit_bytes=56 << 20),
    )(seq_ids, confidence, tokens, out_grad, gate_weight, up_weight, down_weight)


def solution(mesh):
    placed = (
        P("col", "row"),
        P("col", "row"),
        P("col"),
        P(),
        P("row", "col"),
        P("row", "col"),
        P("col", "row"),
    )
    return jax.shard_map(
        local,
        mesh=mesh,
        in_specs=placed,
        out_specs=(P("col", "row"), P("row", "col"), P("row", "col"), P("col", "row")),
        check_vma=False,
    )
```

time: 402 us -> 85.2 us (0.21)
  waiting for transfers between devices: 265 us -> 0 us
  blocking collectives: 79.2 us -> 0 us
  Pallas kernels: 0 us -> 75.5 us
  matrix products: 25.6 us -> 0 us
  between operations: 13.8 us -> 0.64 us
  other arithmetic: 8.8 us -> 0 us
    reduce_scatter x2 -> x0, waiting for transfers between devices: 173 us -> none  [the longest x1 89.2 us: local(): lax.psum_scatter(jnp.concatenate([gate_part, up_part, hidden_part], axis=...]
    all_gather x3 -> x0, waiting for transfers between devices: 90.5 us -> none  [the longest x1 37.4 us: local(): lax.all_gather(grad_pre_gate, 'row', axis=0, tiled=True)]
    all_gather x2 -> x0, blocking collectives: 79.2 us -> none  [the longest x1 43.5 us: local(): lax.all_gather(weighted, 'col', axis=0, tiled=True)]
    pallas_call x0 -> x1, Pallas kernels: none -> 75.5 us  [local(): pl.pallas_call(main_kernel, name='exchange', out_shape=(jax.ShapeDtypeStr...]
    dot_general x9 -> x0, matrix products: 25.6 us -> none  [the longest x3 11.7 us: contract_rows(): lax.dot_general(left, right, (((0,), (0,)), ((), ())), preferred_element_...]
    concatenate x1 -> x0, other arithmetic: 4.51 us -> none  [local(): jnp.concatenate([gate_part, up_part, hidden_part], axis=1)]
    convert_element_type x3 -> x0, other arithmetic: 4.28 us -> none  [the longest x1 1.99 us: pointwise(): hidden = (silu_gate * up).astype(jnp.bfloat16)]
  transfers between devices with their start and end apart: 5 -> 0, of which waited for: 5 -> 0; matrix products, arithmetic and copies ran while one was open for 7% -> 0% of each run, Pallas kernels for 0% -> 0%
where the time goes in v2:
time: 85.2 us; the launch traced here: 83.9 us
  Pallas kernels  75.5 us (89%)
  local copies, waits for them, and re-layouts  7.75 us (9%)
    pallas_call x1, Pallas kernels, local(): pl.pallas_call(main_kernel, name='exchange', out_shape=(jax.ShapeDtypeStr...  75.5 us
    unnamed x8, local copies, waits for them, and re-layouts  7.75 us

profile of v2, /device:TPU:1, one launch (start us, length us, event | category | flops | bytes accessed | tf_op | source)
XLA Modules:
  0.0 83.9 jit_solution(8367241492211359534)
XLA Ops:
  0.6 75.5 %exchange.1 = (bf16[32,512]{1,0:T(8,128)(2,1)}, bf16[512,1792]{1,0:T(8,128)(2,1)}, bf16[512,1792]{1,0:T(8,128)(2,1)}, bf16[1792,512]{1,0:T(8,128)(2,1)}) custom-call(s32[32]{0:T(128)} %seq_hbm.1, s32[8]{0:T(128)} %conf_hbm.1, bf16[32,512]{1,0:T(8,128)(2,1)} %tok_hbm.1, bf16[32,512]{1,0:T(8,128)(2,1)} %grad_hbm.1, bf16[512,1792]{1,0:T(8,128)(2,1)} %gate_hbm.1, ...), custom_call_target="tpu_custom_call" | custom-call | tf_op jit(solution)/shard_map/exchange/pallas_call | solution.py:393
  76.2 1.4 %copy.15 = bf16[32,512]{1,0:T(8,128)(2,1)} copy(bf16[32,512]{1,0:T(8,128)(2,1)} %get-tuple-element.8) | data formatting | bytes 65536
  77.6 0.0 copy-start.1
  77.6 3.0 %copy.16 = bf16[512,1792]{1,0:T(8,128)(2,1)} copy(bf16[512,1792]{1,0:T(8,128)(2,1)} %get-tuple-element.9) | data formatting | bytes 3670016
  80.5 0.0 copy-done.1
  80.6 0.0 copy-start
  80.6 1.2 %copy.17 = bf16[512,1792]{1,0:T(8,128)(2,1)} copy(bf16[512,1792]{1,0:T(8,128)(2,1)S(1)} %copy-done.1) | data formatting | bytes 3670016
  81.8 0.9 %copy-done = bf16[1792,512]{1,0:T(8,128)(2,1)S(1)} copy-done((bf16[1792,512]{1,0:T(8,128)(2,1)S(1)}, bf16[1792,512]{1,0:T(8,128)(2,1)}, u32[]{:S(2)}) %copy-start) | copy-done | bytes 1835032
  82.7 1.2 %copy.18 = bf16[1792,512]{1,0:T(8,128)(2,1)} copy(bf16[1792,512]{1,0:T(8,128)(2,1)S(1)} %copy-done) | data formatting | bytes 3670016
Async XLA Ops:
  77.6 3.0 %copy-start.1 = (bf16[512,1792]{1,0:T(8,128)(2,1)S(1)}, bf16[512,1792]{1,0:T(8,128)(2,1)}, u32[]{:S(2)}) copy-start(bf16[512,1792]{1,0:T(8,128)(2,1)} %get-tuple-element.10) | copy-start | bytes 5505028
  80.6 2.2 %copy-start = (bf16[1792,512]{1,0:T(8,128)(2,1)S(1)}, bf16[1792,512]{1,0:T(8,128)(2,1)}, u32[]{:S(2)}) copy-start(bf16[1792,512]{1,0:T(8,128)(2,1)} %get-tuple-element.11) | copy-start | bytes 5505028

commit v3 on v2

--- a/solution.py
+++ b/solution.py
@@ -10,14 +10,15 @@
 NX, NZ, NH, NY = 4, 2, 4, 4
 CHUNKS = 4
 ORDER = (0, 1, 3, 2)
-NA = 5
+NA = 4
+DIRECT = 0
 SCHEDULE = (
-    "T0", "Z2", "FA0", "FB0", "Z1", "Z3", "MA0", "T2", "SB0", "FA2", "FB2", "T1", "SA0", "MB0", "FA1", "FB1",
-    "T3", "MA2", "SB2", "FA3", "PB0", "FB3", "PA0", "MA1", "SB1", "SA2", "MB2", "SB3", "MA3", "AA0", "WB0",
-    "PA2", "SA1", "MB1", "PB2", "MB3", "SA3", "AA2", "PA1", "WA0", "YB0", "PB1", "WB2", "PA3", "PB3", "AA1",
-    "WA2", "HB0", "HA0", "BA0", "BB0", "YB2", "WB1", "AA3", "WB3", "C0", "WA1", "HB2", "HA2", "BA2", "BB2",
-    "YB1", "D0", "C2", "WA3", "YB3", "HA1", "BA1", "HB1", "BB1", "HA3", "BA3", "D2", "C1", "HB3", "BB3",
-    "G0", "G1", "C3", "G2", "G3", "G4", "D1", "G5", "D3", "E0",
+    "T0", "U0", "Z1", "FA0", "FB0", "Z2", "FH0", "T1", "Z3", "MA0", "SB0", "FB1", "FA1", "FH1", "T2", "MB0",
+    "FA2", "FB2", "FH2", "T3", "MA1", "SB1", "FB3", "FA3", "FH3", "MA2", "SA1", "MB1", "SA0", "SB2", "MA3",
+    "SB3", "SA2", "PB1", "MB2", "PA1", "PB0", "SA3", "MB3", "PA0", "WB1", "PB2", "AA1", "PA2", "PA3", "PB3",
+    "YB1", "WB2", "AA2", "WB3", "AA3", "YB2", "WA1", "YB3", "WA2", "WA3", "HB1", "HB2", "YB0", "HA1", "AA0",
+    "BA1", "HA2", "BB1", "HA3", "BA3", "HB3", "BB3", "C1", "BA2", "BB2", "C3", "C2", "HB0", "HA0", "BA0",
+    "BB0", "D3", "G4", "C0", "D1", "D2", "G0", "G3", "G5", "G1", "G2", "D0", "E0",
 )
 
 def contract_last(left, right):
@@ -39,12 +40,12 @@
 
 def main_kernel(
     seq_hbm, conf_hbm, tok_hbm, grad_hbm, gate_hbm, up_hbm, down_hbm,
-    gtok_ref, gg_hbm, gu_hbm, gd_hbm,
+    gtok_ref, og, ou, od,
     seq, conf, raw, acts, wg, wu, wd, part, full,
     far_a, fin_a, sum_a, mid_a, out_a, in_a, own_a,
     in_b, full_b, part_b, far_b, fin_b, sum_b, mid_b,
-    tot, hb, hs, gp, gq, gr, sd, rd, se, re, own_t, og, ou, od,
-    lsem, osem, wsem, hsem, ysem, csem,
+    tot, hb, hs, gp, gq, gr, sd, rd, se, re, own_t,
+    lsem, wsem, hsem, ysem, csem, ywsem, cwsem,
     far_as, fin_as, sum_as, z_as, gz_as, gx_as, gw_as, sh_as,
     far_bs, fin_bs, sum_bs, z_bs, gz_bs, gx_bs, gw_bs, sh_bs,
     psem, dsem, esem,
@@ -72,8 +73,9 @@
 
     zpeer, speer = dev(z=1 - z), dev(c=sib)
     xpeers = (dev(x=right), dev(x=left))
-
-    sent, kept, state = [], [], {}
+    apeer = dev(x=across)
+
+    sent, state, seen = [], {}, set()
 
     def send(key, src, dst, sems, index, peer):
         copy = pltpu.make_async_remote_copy(
@@ -84,7 +86,9 @@
         state[key] = copy
 
     def wait(key):
-        state[key].wait_recv()
+        if key not in seen:
+            seen.add(key)
+            state[key].wait_recv()
 
     def local(src, dst, sem):
         copy = pltpu.make_async_copy(src, dst, sem)
@@ -92,7 +96,7 @@
         return copy
 
     bar = pltpu.get_barrier_semaphore()
-    peers = list(xpeers) + [ypeer(i) for i in (1, 2, 3)] + [hpeer(i) for i in (1, 2, 3)] + [zpeer, speer]
+    peers = list(xpeers) + [apeer] + [ypeer(i) for i in (1, 2, 3)] + [hpeer(i) for i in (1, 2, 3)] + [zpeer, speer]
     for peer in peers:
         pl.semaphore_signal(bar, inc=1, device_id=peer, device_id_type=MESH)
 
@@ -112,6 +116,13 @@
         local(up_hbm.at[:, mine], wu.at[c], lsem.at[5]),
         local(down_hbm.at[mine, :], wd.at[c], lsem.at[6]),
     ]
+    pl.semaphore_wait(bar, len(peers))
+
+    for i in (1, 3, 2):
+        send(("y", 0, i), tok_hbm, acts.at[c, zh, 0, yrows(0), :], ysem, (0, i - 1), ypeer(i))
+    send(("w", 0), gate_hbm.at[:, theirs], wg.at[c], wsem, (0,), speer)
+    send(("w", 1), up_hbm.at[:, theirs], wu.at[c], wsem, (1,), speer)
+    send(("w", 2), down_hbm.at[theirs, :], wd.at[c], wsem, (2,), speer)
     for copy in first:
         copy.wait()
     at = lax.broadcasted_iota(jnp.int32, (rows, 1), 0)
@@ -119,33 +130,33 @@
     for i in range(rows):
         factor = jnp.where(at == i, conf[seq[i]].astype(F32) * 0.25, factor)
     acts[c, zh, 1, yrows(0), :] = (raw[...].astype(F32) * factor).astype(BF16)
-    pl.semaphore_wait(bar, len(peers))
+    block = acts.at[c, zh, 1, yrows(0), :]
+    for i in (1, 3, 2):
+        send(("yw", i), block, block, ywsem, (i - 1,), ypeer(i))
+    block = acts.at[c, zh, :, yrows(0), :]
+    for i in (1, 3, 2):
+        send(("h", i), block, block, hsem, (i - 1,), hpeer(i))
 
     def plane(k):
         return (zh + ORDER[k]) % NH
 
-    def to_y(k):
+    def pass_y(k):
+        wait(("h", (NH - ORDER[k]) % NH))
         block = acts.at[c, plane(k), :, yrows(0), :]
         for i in (1, 3, 2):
             send(("y", k, i), block, block, ysem, (k, i - 1), ypeer(i))
 
-    to_y(0)
-    block = acts.at[c, zh, :, yrows(0), :]
-    for i in (1, 3, 2):
-        send(("h", i), block, block, hsem, (i - 1,), hpeer(i))
-    send(("w", 0), gate_hbm.at[:, theirs], wg.at[c], wsem, (0,), speer)
-    send(("w", 1), up_hbm.at[:, theirs], wu.at[c], wsem, (1,), speer)
-    send(("w", 2), down_hbm.at[theirs, :], wd.at[c], wsem, (2,), speer)
-
-    def pass_y(k):
-        wait(("h", (NH - ORDER[k]) % NH))
-        to_y(k)
-
     def take(k):
         for i in (1, 3, 2):
             wait(("y", k, i))
-        got = acts.at[c, plane(k)]
+        got = acts.at[c, plane(k)] if k else acts.at[c, zh, 0]
         send(("c", k), got, got, csem, (k,), speer)
+
+    def take_weighted(_):
+        for i in (1, 3, 2):
+            wait(("yw", i))
+        got = acts.at[c, zh, 1]
+        send(("cw",), got, got, cwsem, (), speer)
 
     def product(k, which, lo, n):
         span = pl.ds(lo * 128, n * 128)
@@ -167,23 +178,33 @@
         cut = (n + 1 - k % 2) // 2
         return (0, cut), (cut, n - cut)
 
+    def send_a(k, h):
+        lo, n = halves(ga, k)[h]
+        send(("far_a", k, h), part.at[k, across, :, pl.ds(lo, n)], far_a.at[k, h, :, pl.ds(0, n)],
+             far_as, (k, h), xpeers[h])
+        d = 1 - h
+        send(("fin_a", k, d), part.at[k, (right, left)[d], :, pl.ds(lo, n)],
+             fin_a.at[k, d, :, pl.ds(0, n)], fin_as, (k, d), xpeers[d])
+
+    def ready(k, which):
+        wait(("c", k))
+        if which == 2:
+            wait(("cw",))
+        wait(("w", which))
+        if which not in seen:
+            seen.add(which)
+            loads[which].wait()
+
     def forward_a(k):
-        if k == 0:
-            for copy in loads:
-                copy.wait()
-        wait(("c", k))
-        for which in range(3):
-            if k == 0:
-                wait(("w", which))
+        for which in range(2):
+            ready(k, which)
             product(k, which, 0, NA)
-        for d in range(2):
-            lo, n = halves(ga, k)[d]
-            send(("far_a", k, d), part.at[k, across, :, pl.ds(lo, n)], far_a.at[k, d, :, pl.ds(0, n)],
-                 far_as, (k, d), xpeers[d])
-        for d in range(2):
-            lo, n = halves(ga, k)[1 - d]
-            send(("fin_a", k, d), part.at[k, (right, left)[d], :, pl.ds(lo, n)],
-                 fin_a.at[k, d, :, pl.ds(0, n)], fin_as, (k, d), xpeers[d])
+        send_a(k, 0)
+
+    def forward_h(k):
+        ready(k, 2)
+        product(k, 2, 0, NA)
+        send_a(k, 1)
 
     def middle_a(k):
         for d in range(2):
@@ -226,6 +247,8 @@
         block = hb.at[k, x, :, pl.ds(0, ga)]
         for d in range(2):
             send(("gx_a", k, d), block, block, gx_as, (k, d), xpeers[d])
+        if k == DIRECT:
+            send(("gw_a", k, 0), block, block, gw_as, (k, 0), apeer)
 
     def onward_a(k):
         for d in range(2):
@@ -234,13 +257,18 @@
             block = hb.at[k, (left, right)[d], :, pl.ds(lo, n)]
             send(("gw_a", k, d), block, block, gw_as, (k, d), xpeers[d])
 
+    def arrived(far, near, k):
+        for key in ((near, k, 0), (near, k, 1), (far, k, 0), (far, k, 1)):
+            if key in state:
+                wait(key)
+
     def share_a(k):
-        for d in range(2):
-            wait(("gw_a", k, d))
+        arrived("gw_a", "gx_a", k)
         send(("sh_a", k), hb.at[k, :, :, pl.ds(0, ga)], hs.at[k, :, :, pl.ds(0, ga)], sh_as, (k,), speer)
 
     def forward_b(k):
         for which in range(3):
+            ready(k, which)
             product(k, which, NA, nb)
         send(("z_b", k), part.at[k, :, 1 - z, pl.ds(ga, gb)], in_b.at[k], z_bs, (k,), zpeer)
 
@@ -282,6 +310,8 @@
         block = hb.at[k, x, z, pl.ds(ga, gb)]
         for d in range(2):
             send(("gx_b", k, d), block, block, gx_bs, (k, d), xpeers[d])
+        if k == DIRECT:
+            send(("gw_b", k, 0), block, block, gw_bs, (k, 0), apeer)
 
     def onward_b(k):
         for d in range(2):
@@ -291,8 +321,7 @@
             send(("gw_b", k, d), block, block, gw_bs, (k, d), xpeers[d])
 
     def across_b(k):
-        for d in range(2):
-            wait(("gw_b", k, d))
+        arrived("gw_b", "gx_b", k)
         block = hb.at[k, :, z, pl.ds(ga, gb)]
         send(("gz_b", k), block, block, gz_bs, (k,), zpeer)
 
@@ -347,7 +376,7 @@
     def weight_grads(n):
         ref, half = (hb, c) if n < 3 else (hs, sib)
         which = (1, 2, 0)[n % 3]
-        if n == 3:
+        if n >= 3:
             for k in range(CHUNKS):
                 wait(("sh_a", k))
                 wait(("sh_b", k))
@@ -358,21 +387,26 @@
         span = pl.ds(pl.multiple_of(half * width, 128), width)
         if which == 0:
             od[span, :] = contract_first(units, acted).astype(BF16)
-            kept.append(local(od.at[span, :], gd_hbm.at[span, :], osem.at[n]))
         else:
-            out, hbm = ((og, gg_hbm), (ou, gu_hbm))[which - 1]
-            out[:, span] = contract_first(acted, units).astype(BF16)
-            kept.append(local(out.at[:, span], hbm.at[:, span], osem.at[n]))
+            (og, ou)[which - 1][:, span] = contract_first(acted, units).astype(BF16)
 
     stages = dict(
-        Z=pass_y, T=take, FA=forward_a, FB=forward_b, MA=middle_a, SA=second_a, PA=point_a, AA=across_a,
+        Z=pass_y, T=take, U=take_weighted, FA=forward_a, FH=forward_h, FB=forward_b, MA=middle_a, SA=second_a, PA=point_a, AA=across_a,
         WA=onward_a, HA=share_a, SB=second_b, MB=middle_b, PB=point_b, WB=onward_b, YB=across_b,
         HB=share_b, BA=back_a, BB=back_b, C=cols_send, D=cols_sum, E=finish, G=weight_grads)
     for item in SCHEDULE:
         stages[item[:-1]](int(item[-1]))
     for copy in sent:
         copy.wait_send()
-    for copy in kept:
+
+
+def write_kernel(*refs):
+    n = len(refs) // 2
+    sem = refs[-1]
+    copies = [pltpu.make_async_copy(refs[i], refs[n + i], sem.at[i]) for i in range(n)]
+    for copy in copies:
+        copy.start()
+    for copy in copies:
         copy.wait()
 
 
@@ -390,17 +424,13 @@
     anyspace = pl.BlockSpec(memory_space=pl.ANY)
     vmspace = pl.BlockSpec(memory_space=pltpu.VMEM)
     one, two = dma((2, k)), dma((2, k, 2))
-    return pl.pallas_call(
+    shapes = (rows, depth), (depth, 2 * width), (depth, 2 * width), (2 * width, depth)
+    results = pl.pallas_call(
         main_kernel,
         name="exchange",
-        out_shape=(
-            jax.ShapeDtypeStruct((rows, depth), BF16),
-            jax.ShapeDtypeStruct((depth, 2 * width), BF16),
-            jax.ShapeDtypeStruct((depth, 2 * width), BF16),
-            jax.ShapeDtypeStruct((2 * width, depth), BF16),
-        ),
+        out_shape=tuple(vm(shape, BF16) for shape in shapes),
         in_specs=[anyspace] * 7,
-        out_specs=(vmspace, anyspace, anyspace, anyspace),
+        out_specs=(vmspace,) * 4,
         scratch_shapes=[
             sm(seq_ids.shape, jnp.int32),
             sm(confidence.shape, jnp.int32),
@@ -436,17 +466,24 @@
             vm((3, rows, depth), BF16),
             vm((3, rows, depth), BF16),
             vm((rows, depth), F32),
-            vm((depth, 2 * width), BF16),
-            vm((depth, 2 * width), BF16),
-            vm((2 * width, depth), BF16),
-            dma((7,)), dma((6,)), dma((2, 3)), dma((2, 3)), dma((2, k, 3)), one,
+            dma((7,)), dma((2, 3)), dma((2, 3)), dma((2, k, 3)), one, dma((2, 3)), dma((2,)),
             two, two, two, one, one, two, two, one,
             two, two, two, one, one, two, two, one,
             one, dma((2, k, 3)), dma((2, 3)),
         ],
         compiler_params=pltpu.CompilerParams(
-            collective_id=0, has_side_effects=True, vmem_limit_bytes=56 << 20),
-    )(seq_ids, confidence, tokens, out_grad, gate_weight, up_weight, down_weight)
+            collective_id=0, has_side_effects=True, vmem_limit_bytes=48 << 20),
+    )(*(pltpu.with_memory_space_constraint(v, pltpu.HBM) for v in (
+        seq_ids, confidence, tokens, out_grad, gate_weight, up_weight, down_weight)))
+    return pl.pallas_call(
+        write_kernel,
+        name="write_out",
+        out_shape=tuple(jax.ShapeDtypeStruct(shape, BF16) for shape in shapes),
+        in_specs=[vmspace] * 4,
+        out_specs=(anyspace,) * 4,
+        scratch_shapes=[dma((4,))],
+        compiler_params=pltpu.CompilerParams(vmem_limit_bytes=16 << 20),
+    )(*(pltpu.with_memory_space_constraint(v, pltpu.VMEM) for v in results))
 
 
 def solution(mesh):

time: 85.2 us -> 74.4 us (0.87); the launches traced: 83.9 us -> 74.1 us
  local copies, waits for them, and re-layouts: 7.75 us -> 0 us
  Pallas kernels: 75.5 us -> 73.4 us
    unnamed x8 -> x0, local copies, waits for them, and re-layouts: 7.75 us -> none
    pallas_call x1 -> x2, Pallas kernels: 75.5 us -> 73.4 us  [the longest x1 70.9 us: local(): pl.pallas_call(main_kernel, name='exchange', out_shape=tuple((vm(shape, B...]
where the time goes in v3:
time: 74.4 us; the launch traced here: 74.1 us
  Pallas kernels  73.4 us (99%)
    pallas_call x1, Pallas kernels, local(): pl.pallas_call(main_kernel, name='exchange', out_shape=tuple((vm(shape, B...  70.9 us
    pallas_call x1, Pallas kernels, local(): pl.pallas_call(write_kernel, name='write_out', out_shape=tuple((jax.Shape...  2.48 us

profile of v3, /device:TPU:1, one launch (start us, length us, event | category | flops | bytes accessed | tf_op | source)
XLA Modules:
  0.0 74.1 jit_solution(16533356466819040757)
XLA Ops:
  0.6 70.9 %exchange.1 = (bf16[32,512]{1,0:T(8,128)(2,1)S(1)}, bf16[512,1792]{1,0:T(8,128)(2,1)S(1)}, bf16[512,1792]{1,0:T(8,128)(2,1)S(1)}, bf16[1792,512]{1,0:T(8,128)(2,1)S(1)}) custom-call(s32[32]{0:T(128)} %seq_hbm.1, s32[8]{0:T(128)} %conf_hbm.1, bf16[32,512]{1,0:T(8,128)(2,1)} %tok_hbm.1, bf16[32,512]{1,0:T(8,128)(2,1)} %grad_hbm.1, bf16[512,1792]{1,0:T(8,128)(2,1)} %gate_hbm.1, ...), custom_call_target="tpu_custom_call" | custom-call | tf_op jit(solution)/shard_map/exchange/pallas_call | solution.py:428
  71.6 2.5 %write_out.1 = (bf16[32,512]{1,0:T(8,128)(2,1)}, bf16[512,1792]{1,0:T(8,128)(2,1)}, bf16[512,1792]{1,0:T(8,128)(2,1)}, bf16[1792,512]{1,0:T(8,128)(2,1)}) custom-call(bf16[32,512]{1,0:T(8,128)(2,1)S(1)} %get-tuple-element.8.refs_0_, bf16[512,1792]{1,0:T(8,128)(2,1)S(1)} %get-tuple-element.9.refs_1_, bf16[512,1792]{1,0:T(8,128)(2,1)S(1)} %get-tuple-element.10.refs_2_, ...), custom_call_target="tpu_custom_call" | custom-call | tf_op jit(solution)/shard_map/write_out/pallas_call | solution.py:478

commit v4 on v3

--- a/solution.py
+++ b/solution.py
@@ -13,12 +13,13 @@
 NA = 4
 DIRECT = 0
 SCHEDULE = (
-    "T0", "U0", "Z1", "FA0", "FB0", "Z2", "FH0", "T1", "Z3", "MA0", "SB0", "FB1", "FA1", "FH1", "T2", "MB0",
-    "FA2", "FB2", "FH2", "T3", "MA1", "SB1", "FB3", "FA3", "FH3", "MA2", "SA1", "MB1", "SA0", "SB2", "MA3",
-    "SB3", "SA2", "PB1", "MB2", "PA1", "PB0", "SA3", "MB3", "PA0", "WB1", "PB2", "AA1", "PA2", "PA3", "PB3",
-    "YB1", "WB2", "AA2", "WB3", "AA3", "YB2", "WA1", "YB3", "WA2", "WA3", "HB1", "HB2", "YB0", "HA1", "AA0",
-    "BA1", "HA2", "BB1", "HA3", "BA3", "HB3", "BB3", "C1", "BA2", "BB2", "C3", "C2", "HB0", "HA0", "BA0",
-    "BB0", "D3", "G4", "C0", "D1", "D2", "G0", "G3", "G5", "G1", "G2", "D0", "E0",
+    "Z2", "T0", "Z1", "U0", "FA0", "V2", "Z3", "FH0", "FB0", "T2", "V3", "T1", "FA2", "V1", "U2", "MA0",
+    "FA1", "FB2", "T3", "FH2", "U3", "SB0", "FA3", "FB3", "U1", "FH3", "MA2", "FH1", "FB1", "SB2", "MA3",
+    "MA1", "SA2", "SA0", "MB2", "SB3", "MB0", "SA3", "SB1", "SA1", "PB2", "PA2", "MB3", "MB1", "PA3", "PA1",
+    "WB2", "PB3", "AA2", "PB1", "AA3", "YB2", "WB3", "AA1", "WA2", "WB1", "WA3", "HB2", "YB3", "PB0", "WA1",
+    "PA0", "HA2", "BA2", "YB1", "BB2", "HB3", "HA3", "BA3", "BB3", "WB0", "C2", "AA0", "YB0", "HB1", "HA1",
+    "BA1", "BB1", "C3", "C1", "HB0", "BB0", "HA0", "BA0", "D3", "D2", "C0", "D1", "G2", "G1", "G0", "G3",
+    "G5", "G4", "D0", "E0",
 )
 
 def contract_last(left, right):
@@ -45,7 +46,7 @@
     far_a, fin_a, sum_a, mid_a, out_a, in_a, own_a,
     in_b, full_b, part_b, far_b, fin_b, sum_b, mid_b,
     tot, hb, hs, gp, gq, gr, sd, rd, se, re, own_t,
-    lsem, wsem, hsem, ysem, csem, ywsem, cwsem,
+    lsem, wsem, hsem, ysem, csem,
     far_as, fin_as, sum_as, z_as, gz_as, gx_as, gw_as, sh_as,
     far_bs, fin_bs, sum_bs, z_bs, gz_bs, gx_bs, gw_bs, sh_bs,
     psem, dsem, esem,
@@ -75,7 +76,7 @@
     xpeers = (dev(x=right), dev(x=left))
     apeer = dev(x=across)
 
-    sent, state, seen = [], {}, set()
+    sent, state, seen, begun = [], {}, set(), set()
 
     def send(key, src, dst, sems, index, peer):
         copy = pltpu.make_async_remote_copy(
@@ -118,8 +119,22 @@
     ]
     pl.semaphore_wait(bar, len(peers))
 
-    for i in (1, 3, 2):
-        send(("y", 0, i), tok_hbm, acts.at[c, zh, 0, yrows(0), :], ysem, (0, i - 1), ypeer(i))
+    def plane(k):
+        return (zh + ORDER[k]) % NH
+
+    def block_of(k, arr):
+        return acts.at[c, plane(k), arr, yrows(0), :]
+
+    def to_y(k, arr, src):
+        for i in (1, 3, 2):
+            send(("y", arr, k, i), src, block_of(k, arr), ysem, (arr, k, i - 1), ypeer(i))
+
+    def to_h(arr, src):
+        for i in (1, 3, 2):
+            send(("h", arr, i), src, block_of(0, arr), hsem, (arr, i - 1), hpeer(i))
+
+    to_y(0, 0, tok_hbm)
+    to_h(0, tok_hbm)
     send(("w", 0), gate_hbm.at[:, theirs], wg.at[c], wsem, (0,), speer)
     send(("w", 1), up_hbm.at[:, theirs], wu.at[c], wsem, (1,), speer)
     send(("w", 2), down_hbm.at[theirs, :], wd.at[c], wsem, (2,), speer)
@@ -130,33 +145,24 @@
     for i in range(rows):
         factor = jnp.where(at == i, conf[seq[i]].astype(F32) * 0.25, factor)
     acts[c, zh, 1, yrows(0), :] = (raw[...].astype(F32) * factor).astype(BF16)
-    block = acts.at[c, zh, 1, yrows(0), :]
-    for i in (1, 3, 2):
-        send(("yw", i), block, block, ywsem, (i - 1,), ypeer(i))
-    block = acts.at[c, zh, :, yrows(0), :]
-    for i in (1, 3, 2):
-        send(("h", i), block, block, hsem, (i - 1,), hpeer(i))
-
-    def plane(k):
-        return (zh + ORDER[k]) % NH
-
-    def pass_y(k):
-        wait(("h", (NH - ORDER[k]) % NH))
-        block = acts.at[c, plane(k), :, yrows(0), :]
+    to_y(0, 1, block_of(0, 1))
+    to_h(1, block_of(0, 1))
+
+    def pass_y(k, arr=0):
+        wait(("h", arr, (NH - ORDER[k]) % NH))
+        to_y(k, arr, block_of(k, arr))
+
+    def pass_weighted(k):
+        pass_y(k, 1)
+
+    def take(k, arr=0):
         for i in (1, 3, 2):
-            send(("y", k, i), block, block, ysem, (k, i - 1), ypeer(i))
-
-    def take(k):
-        for i in (1, 3, 2):
-            wait(("y", k, i))
-        got = acts.at[c, plane(k)] if k else acts.at[c, zh, 0]
-        send(("c", k), got, got, csem, (k,), speer)
-
-    def take_weighted(_):
-        for i in (1, 3, 2):
-            wait(("yw", i))
-        got = acts.at[c, zh, 1]
-        send(("cw",), got, got, cwsem, (), speer)
+            wait(("y", arr, k, i))
+        got = acts.at[c, plane(k), arr]
+        send(("c", arr, k), got, got, csem, (arr, k), speer)
+
+    def take_weighted(k):
+        take(k, 1)
 
     def product(k, which, lo, n):
         span = pl.ds(lo * 128, n * 128)
@@ -187,9 +193,7 @@
              fin_a.at[k, d, :, pl.ds(0, n)], fin_as, (k, d), xpeers[d])
 
     def ready(k, which):
-        wait(("c", k))
-        if which == 2:
-            wait(("cw",))
+        wait(("c", 1 if which == 2 else 0, k))
         wait(("w", which))
         if which not in seen:
             seen.add(which)
@@ -241,29 +245,31 @@
             hb[k, x, z, which * NA : (which + 1) * NA] = results[which]
         block = hb.at[k, x, z, pl.ds(0, ga)]
         send(("gz_a", k), block, block, gz_as, (k,), zpeer)
+        along_x(k, block, 0)
+
+    def along_x(k, block, part_of):
+        for d in range(2):
+            send(("gx_a", k, d, part_of), block, block, gx_as, (k, d, part_of), xpeers[d])
+        if k == DIRECT:
+            send(("gw_a", k, part_of), block, block, gw_as, (k, part_of), apeer)
 
     def across_a(k):
         wait(("gz_a", k))
-        block = hb.at[k, x, :, pl.ds(0, ga)]
-        for d in range(2):
-            send(("gx_a", k, d), block, block, gx_as, (k, d), xpeers[d])
-        if k == DIRECT:
-            send(("gw_a", k, 0), block, block, gw_as, (k, 0), apeer)
+        along_x(k, hb.at[k, x, 1 - z, pl.ds(0, ga)], 1)
 
     def onward_a(k):
         for d in range(2):
             lo, n = halves(ga, k)[d]
-            wait(("gx_a", k, d))
+            for part_of in range(2):
+                wait(("gx_a", k, d, part_of))
             block = hb.at[k, (left, right)[d], :, pl.ds(lo, n)]
             send(("gw_a", k, d), block, block, gw_as, (k, d), xpeers[d])
 
-    def arrived(far, near, k):
-        for key in ((near, k, 0), (near, k, 1), (far, k, 0), (far, k, 1)):
-            if key in state:
-                wait(key)
-
     def share_a(k):
-        arrived("gw_a", "gx_a", k)
+        for d in range(2):
+            for part_of in range(2):
+                wait(("gx_a", k, d, part_of))
+            wait(("gw_a", k, d))
         send(("sh_a", k), hb.at[k, :, :, pl.ds(0, ga)], hs.at[k, :, :, pl.ds(0, ga)], sh_as, (k,), speer)
 
     def forward_b(k):
@@ -310,23 +316,30 @@
         block = hb.at[k, x, z, pl.ds(ga, gb)]
         for d in range(2):
             send(("gx_b", k, d), block, block, gx_bs, (k, d), xpeers[d])
+        send(("gz_b", k, 0), block, block, gz_bs, (k, 0), zpeer)
         if k == DIRECT:
             send(("gw_b", k, 0), block, block, gw_bs, (k, 0), apeer)
 
     def onward_b(k):
         for d in range(2):
-            lo, n = halves(gb, k)[d]
             wait(("gx_b", k, d))
-            block = hb.at[k, (left, right)[d], z, pl.ds(ga + lo, n)]
-            send(("gw_b", k, d), block, block, gw_bs, (k, d), xpeers[d])
+            if k != DIRECT:
+                lo, n = halves(gb, k)[d]
+                block = hb.at[k, (left, right)[d], z, pl.ds(ga + lo, n)]
+                send(("gw_b", k, d), block, block, gw_bs, (k, d), xpeers[d])
+        for d in range(2):
+            block = hb.at[k, (left, right)[d], z, pl.ds(ga, gb)]
+            send(("gz_b", k, 1 + d), block, block, gz_bs, (k, 1 + d), zpeer)
 
     def across_b(k):
-        arrived("gw_b", "gx_b", k)
-        block = hb.at[k, :, z, pl.ds(ga, gb)]
-        send(("gz_b", k), block, block, gz_bs, (k,), zpeer)
+        for d in range(1 if k == DIRECT else 2):
+            wait(("gw_b", k, d))
+        block = hb.at[k, across, z, pl.ds(ga, gb)]
+        send(("gz_b", k, 3), block, block, gz_bs, (k, 3), zpeer)
 
     def share_b(k):
-        wait(("gz_b", k))
+        for i in range(4):
+            wait(("gz_b", k, i))
         send(("sh_b", k), hb.at[k, :, :, pl.ds(ga, gb)], hs.at[k, :, :, pl.ds(ga, gb)], sh_bs, (k,), speer)
 
     def flat(ref, k, first, n):
@@ -336,16 +349,19 @@
         dg = jnp.concatenate(flat(hb, k, base + n, n), axis=1)
         du = jnp.concatenate(flat(hb, k, base + 2 * n, n), axis=1)
         span = pl.ds(lo * 128, n * 128)
-        return [contract_last(dg, wg[h, :, span]) + contract_last(du, wu[h, :, span]) for h in (sib, c)]
+        again = k in begun
+        begun.add(k)
+        for h, ref in ((sib, gq), (c, gp)):
+            value = contract_last(dg, wg[h, :, span]) + contract_last(du, wu[h, :, span])
+            ref[k] = ref[k] + value if again else value
+            if again and ref is gq:
+                send(("p", k), gq.at[k], gr.at[k], psem, (k,), speer)
 
     def back_a(k):
-        gq[k], gp[k] = back(k, 0, 0, NA)
+        back(k, 0, 0, NA)
 
     def back_b(k):
-        other, own = back(k, ga, NA, nb)
-        gq[k] = gq[k] + other
-        send(("p", k), gq.at[k], gr.at[k], psem, (k,), speer)
-        gp[k] = gp[k] + own
+        back(k, ga, NA, nb)
 
     def cols_send(k):
         wait(("p", k))
@@ -391,10 +407,14 @@
             (og, ou)[which - 1][:, span] = contract_first(acted, units).astype(BF16)
 
     stages = dict(
-        Z=pass_y, T=take, U=take_weighted, FA=forward_a, FH=forward_h, FB=forward_b, MA=middle_a, SA=second_a, PA=point_a, AA=across_a,
+        Z=pass_y, V=pass_weighted, T=take, U=take_weighted, FA=forward_a, FH=forward_h, FB=forward_b, MA=middle_a, SA=second_a, PA=point_a, AA=across_a,
         WA=onward_a, HA=share_a, SB=second_b, MB=middle_b, PB=point_b, WB=onward_b, YB=across_b,
         HB=share_b, BA=back_a, BB=back_b, C=cols_send, D=cols_sum, E=finish, G=weight_grads)
     for item in SCHEDULE:
+        for copy in sent[:4]:
+            if len(sent) > 30:
+                sent.remove(copy)
+                copy.wait_send()
         stages[item[:-1]](int(item[-1]))
     for copy in sent:
         copy.wait_send()
@@ -466,9 +486,9 @@
             vm((3, rows, depth), BF16),
             vm((3, rows, depth), BF16),
             vm((rows, depth), F32),
-            dma((7,)), dma((2, 3)), dma((2, 3)), dma((2, k, 3)), one, dma((2, 3)), dma((2,)),
-            two, two, two, one, one, two, two, one,
-            two, two, two, one, one, two, two, one,
+            dma((7,)), dma((2, 3)), dma((2, 2, 3)), dma((2, 2, k, 3)), dma((2, 2, k)),
+            two, two, two, one, one, dma((2, k, 2, 2)), two, one,
+            two, two, two, one, dma((2, k, 4)), two, two, one,
             one, dma((2, k, 3)), dma((2, 3)),
         ],
         compiler_params=pltpu.CompilerParams(

time: 74.4 us -> 72.9 us (0.980)
  Pallas kernels: 73.4 us -> 72.2 us
    pallas_call x1, Pallas kernels: 70.9 us -> 69.7 us  [local(): pl.pallas_call(main_kernel, name='exchange', out_shape=tuple((vm(shape, B...]
where the time goes in v4:
time: 72.9 us; the launch traced here: 72.8 us
  Pallas kernels  72.2 us (99%)
    pallas_call x1, Pallas kernels, local(): pl.pallas_call(main_kernel, name='exchange', out_shape=tuple((vm(shape, B...  69.7 us
    pallas_call x1, Pallas kernels, local(): pl.pallas_call(write_kernel, name='write_out', out_shape=tuple((jax.Shape...  2.48 us

profile of v4, /device:TPU:1, one launch (start us, length us, event | category | flops | bytes accessed | tf_op | source)
XLA Modules:
  0.0 72.8 jit_solution(481868422025209051)
XLA Ops:
  0.6 69.7 %exchange.1 = (bf16[32,512]{1,0:T(8,128)(2,1)S(1)}, bf16[512,1792]{1,0:T(8,128)(2,1)S(1)}, bf16[512,1792]{1,0:T(8,128)(2,1)S(1)}, bf16[1792,512]{1,0:T(8,128)(2,1)S(1)}) custom-call(s32[32]{0:T(128)} %seq_hbm.1, s32[8]{0:T(128)} %conf_hbm.1, bf16[32,512]{1,0:T(8,128)(2,1)} %tok_hbm.1, bf16[32,512]{1,0:T(8,128)(2,1)} %grad_hbm.1, bf16[512,1792]{1,0:T(8,128)(2,1)} %gate_hbm.1, ...), custom_call_target="tpu_custom_call" | custom-call | tf_op jit(solution)/shard_map/exchange/pallas_call | solution.py:448
  70.4 2.5 %write_out.1 = (bf16[32,512]{1,0:T(8,128)(2,1)}, bf16[512,1792]{1,0:T(8,128)(2,1)}, bf16[512,1792]{1,0:T(8,128)(2,1)}, bf16[1792,512]{1,0:T(8,128)(2,1)}) custom-call(bf16[32,512]{1,0:T(8,128)(2,1)S(1)} %get-tuple-element.8.refs_0_, bf16[512,1792]{1,0:T(8,128)(2,1)S(1)} %get-tuple-element.9.refs_1_, bf16[512,1792]{1,0:T(8,128)(2,1)S(1)} %get-tuple-element.10.refs_2_, ...), custom_call_target="tpu_custom_call" | custom-call | tf_op jit(solution)/shard_map/write_out/pallas_call | solution.py:498

commit v5 on v4

--- a/solution.py
+++ b/solution.py
@@ -9,17 +9,17 @@
 BF16, F32 = jnp.bfloat16, jnp.float32
 NX, NZ, NH, NY = 4, 2, 4, 4
 CHUNKS = 4
-ORDER = (0, 1, 3, 2)
+ORDER = (0, 3, 1, 2)
 NA = 4
 DIRECT = 0
 SCHEDULE = (
-    "Z2", "T0", "Z1", "U0", "FA0", "V2", "Z3", "FH0", "FB0", "T2", "V3", "T1", "FA2", "V1", "U2", "MA0",
-    "FA1", "FB2", "T3", "FH2", "U3", "SB0", "FA3", "FB3", "U1", "FH3", "MA2", "FH1", "FB1", "SB2", "MA3",
-    "MA1", "SA2", "SA0", "MB2", "SB3", "MB0", "SA3", "SB1", "SA1", "PB2", "PA2", "MB3", "MB1", "PA3", "PA1",
-    "WB2", "PB3", "AA2", "PB1", "AA3", "YB2", "WB3", "AA1", "WA2", "WB1", "WA3", "HB2", "YB3", "PB0", "WA1",
-    "PA0", "HA2", "BA2", "YB1", "BB2", "HB3", "HA3", "BA3", "BB3", "WB0", "C2", "AA0", "YB0", "HB1", "HA1",
-    "BA1", "BB1", "C3", "C1", "HB0", "BB0", "HA0", "BA0", "D3", "D2", "C0", "D1", "G2", "G1", "G0", "G3",
-    "G5", "G4", "D0", "E0",
+    "Z1", "T0", "Z2", "U0", "FA0", "V1", "FH0", "Z3", "FB0", "T1", "V3", "V2", "T2", "MA0", "FA1", "U1",
+    "FA2", "T3", "FB1", "FH1", "U3", "FA3", "FH3", "U2", "FB3", "MA1", "FH2", "SB1", "FB2", "MA3", "SB0",
+    "MB1", "MA2", "SA1", "SB3", "SA3", "MB0", "PB1", "SB2", "SA2", "MB3", "PA1", "PA3", "WB1", "MB2", "PB3",
+    "PA2", "AA3", "YB1", "PB2", "SA0", "WB3", "AA1", "AA2", "WA3", "HB1", "YB3", "WB2", "WA1", "PB0", "WA2",
+    "PA0", "HA3", "BA3", "HB3", "BB3", "HA1", "YB2", "BA1", "WB0", "C3", "BB1", "AA0", "YB0", "HA2", "BA2",
+    "HB2", "BB2", "C1", "C2", "HB0", "BB0", "D3", "HA0", "BA0", "G1", "D1", "C0", "D2", "G5", "G4", "G0",
+    "G2", "G3", "D0", "E0",
 )
 
 def contract_last(left, right):

time: 72.9 us -> 73.4 us (level)
  no operation moved by 1% of the time
where the time goes in v5:
time: 73.4 us; the launch traced here: 73.3 us
  Pallas kernels  72.7 us (99%)
    pallas_call x1, Pallas kernels, local(): pl.pallas_call(main_kernel, name='exchange', out_shape=tuple((vm(shape, B...  70.2 us
    pallas_call x1, Pallas kernels, local(): pl.pallas_call(write_kernel, name='write_out', out_shape=tuple((jax.Shape...  2.48 us

profile of v5, /device:TPU:1, one launch (start us, length us, event | category | flops | bytes accessed | tf_op | source)
XLA Modules:
  0.0 73.3 jit_solution(3224976794033120079)
XLA Ops:
  0.6 70.2 %exchange.1 = (bf16[32,512]{1,0:T(8,128)(2,1)S(1)}, bf16[512,1792]{1,0:T(8,128)(2,1)S(1)}, bf16[512,1792]{1,0:T(8,128)(2,1)S(1)}, bf16[1792,512]{1,0:T(8,128)(2,1)S(1)}) custom-call(s32[32]{0:T(128)} %seq_hbm.1, s32[8]{0:T(128)} %conf_hbm.1, bf16[32,512]{1,0:T(8,128)(2,1)} %tok_hbm.1, bf16[32,512]{1,0:T(8,128)(2,1)} %grad_hbm.1, bf16[512,1792]{1,0:T(8,128)(2,1)} %gate_hbm.1, ...), custom_call_target="tpu_custom_call" | custom-call | tf_op jit(solution)/shard_map/exchange/pallas_call | solution.py:448
  70.8 2.5 %write_out.1 = (bf16[32,512]{1,0:T(8,128)(2,1)}, bf16[512,1792]{1,0:T(8,128)(2,1)}, bf16[512,1792]{1,0:T(8,128)(2,1)}, bf16[1792,512]{1,0:T(8,128)(2,1)}) custom-call(bf16[32,512]{1,0:T(8,128)(2,1)S(1)} %get-tuple-element.8.refs_0_, bf16[512,1792]{1,0:T(8,128)(2,1)S(1)} %get-tuple-element.9.refs_1_, bf16[512,1792]{1,0:T(8,128)(2,1)S(1)} %get-tuple-element.10.refs_2_, ...), custom_call_target="tpu_custom_call" | custom-call | tf_op jit(solution)/shard_map/write_out/pallas_call | solution.py:498
